TPU v7x, 32 devices: a whole 2x2x4 slice. The times are simulated.
32 devices in a mesh: ulysses: 4 (over x, core), blk: 8 (over z, y).
Axes of the slice: x: 2, y: 2, z: 4, core: 2. Of those that a mesh axis runs over, the one named last changes fastest.
Arguments:
- hidden_in: bfloat16 [4096, 1536], P(('ulysses', 'blk')), may hold values from -6 to 6
- out_grad: bfloat16 [4096, 1536], P(('ulysses', 'blk')), may hold values from -6 to 6
- segments: int32 [4096], replicated, may hold values from 0 to 2, as said below
- positions: int32 [4096], replicated, may hold values from 0 to 3582, as said below
- query_master: float32 [1536, 1536], P(('ulysses', 'blk')), may hold values from -0.15625 to 0.15625
- query_first: float32 [1536, 1536], P(('ulysses', 'blk')), may hold values from -9.1552734e-05 to 9.1552734e-05
- query_second: float32 [1536, 1536], P(('ulysses', 'blk')), may hold values from 1.2822512e-11 to 1.2822512e-10
- key_master: float32 [1536, 256], P(('ulysses', 'blk')), may hold values from -0.15625 to 0.15625
- key_first: float32 [1536, 256], P(('ulysses', 'blk')), may hold values from -9.1552734e-05 to 9.1552734e-05
- key_second: float32 [1536, 256], P(('ulysses', 'blk')), may hold values from 1.2822512e-11 to 1.2822512e-10
- value_master: float32 [1536, 256], P(('ulysses', 'blk')), may hold values from -0.15625 to 0.15625
- value_first: float32 [1536, 256], P(('ulysses', 'blk')), may hold values from -9.1552734e-05 to 9.1552734e-05
- value_second: float32 [1536, 256], P(('ulysses', 'blk')), may hold values from 1.2822512e-11 to 1.2822512e-10
- output_master: float32 [1536, 1536], P(None, ('ulysses', 'blk')), may hold values from -3.5 to 3.5
- output_first: float32 [1536, 1536], P(None, ('ulysses', 'blk')), may hold values from -9.1552734e-05 to 9.1552734e-05
- output_second: float32 [1536, 1536], P(None, ('ulysses', 'blk')), may hold values from 1.2822512e-11 to 1.2822512e-10
- gate_master: float32 [1536, 8960], P('blk', 'ulysses'), may hold values from -0.15625 to 0.15625
- gate_first: float32 [1536, 8960], P('blk', 'ulysses'), may hold values from -9.1552734e-05 to 9.1552734e-05
- gate_second: float32 [1536, 8960], P('blk', 'ulysses'), may hold values from 1.2822512e-11 to 1.2822512e-10
- up_master: float32 [1536, 8960], P('blk', 'ulysses'), may hold values from -0.15625 to 0.15625
- up_first: float32 [1536, 8960], P('blk', 'ulysses'), may hold values from -9.1552734e-05 to 9.1552734e-05
- up_second: float32 [1536, 8960], P('blk', 'ulysses'), may hold values from 1.2822512e-11 to 1.2822512e-10
- down_master: float32 [8960, 1536], P('ulysses', 'blk'), may hold values from -0.0625 to 0.0625
- down_first: float32 [8960, 1536], P('ulysses', 'blk'), may hold values from -9.1552734e-05 to 9.1552734e-05
- down_second: float32 [8960, 1536], P('ulysses', 'blk'), may hold values from 1.2822512e-11 to 1.2822512e-10
- small_master: float32 [5120], P(('ulysses', 'blk')), may hold values from -3 to 3
- small_first: float32 [5120], P(('ulysses', 'blk')), may hold values from -0.00036621094 to 0.00036621094
- small_second: float32 [5120], P(('ulysses', 'blk')), may hold values from 2.051602e-10 to 2.051602e-09
Outputs:
- mixed: bfloat16 [4096, 1536], P(('ulysses', 'blk'))
- input_grad: float32 [4096, 1536], P(('ulysses', 'blk'))
- grad_norm: float32 [], replicated
- query_new: float32 [1536, 1536], P(('ulysses', 'blk'))
- query_first_new: float32 [1536, 1536], P(('ulysses', 'blk'))
- query_second_new: float32 [1536, 1536], P(('ulysses', 'blk'))
- query_copy: bfloat16 [1536, 1536], P(('ulysses', 'blk'))
- key_new: float32 [1536, 256], P(('ulysses', 'blk'))
- key_first_new: float32 [1536, 256], P(('ulysses', 'blk'))
- key_second_new: float32 [1536, 256], P(('ulysses', 'blk'))
- key_copy: bfloat16 [1536, 256], P(('ulysses', 'blk'))
- value_new: float32 [1536, 256], P(('ulysses', 'blk'))
- value_first_new: float32 [1536, 256], P(('ulysses', 'blk'))
- value_second_new: float32 [1536, 256], P(('ulysses', 'blk'))
- value_copy: bfloat16 [1536, 256], P(('ulysses', 'blk'))
- output_new: float32 [1536, 1536], P(None, ('ulysses', 'blk'))
- output_first_new: float32 [1536, 1536], P(None, ('ulysses', 'blk'))
- output_second_new: float32 [1536, 1536], P(None, ('ulysses', 'blk'))
- output_copy: bfloat16 [1536, 1536], P(None, ('ulysses', 'blk'))
- gate_new: float32 [1536, 8960], P('blk', 'ulysses')
- gate_first_new: float32 [1536, 8960], P('blk', 'ulysses')
- gate_second_new: float32 [1536, 8960], P('blk', 'ulysses')
- gate_copy: bfloat16 [1536, 8960], P('blk', 'ulysses')
- up_new: float32 [1536, 8960], P('blk', 'ulysses')
- up_first_new: float32 [1536, 8960], P('blk', 'ulysses')
- up_second_new: float32 [1536, 8960], P('blk', 'ulysses')
- up_copy: bfloat16 [1536, 8960], P('blk', 'ulysses')
- down_new: float32 [8960, 1536], P('ulysses', 'blk')
- down_first_new: float32 [8960, 1536], P('ulysses', 'blk')
- down_second_new: float32 [8960, 1536], P('ulysses', 'blk')
- down_copy: bfloat16 [8960, 1536], P('ulysses', 'blk')
- small_new: float32 [5120], P(('ulysses', 'blk'))
- small_first_new: float32 [5120], P(('ulysses', 'blk'))
- small_second_new: float32 [5120], P(('ulysses', 'blk'))
- small_copy: bfloat16 [5120], P(('ulysses', 'blk'))
Inputs may be any that keep to these rules, and one draw needn't show every extreme that they name: Tokens are in order: the prompt of 2048 tokens first (segment 0), then 2 continuations, segments 1 to 2, each one run of 513 to 1535 tokens. `positions`: the prompt counts from 0; each continuation counts from 2048.
All inputs are finite; a program needn't handle non-finite values.
Results may differ from a plain program's by a relative error of at most 0.019.
Values may be sent and summed in bfloat16 or wider, within the bound.
No kernel may reach another device: no remote copies, remote signals or barrier semaphores. Data moves between devices by JAX's collectives and lax.ppermute only.
A program may use at most 192 MiB of HBM per device.

v0:
```python
import math

import jax
import jax.numpy as jnp
from jax import lax
from jax.sharding import PartitionSpec as P

D = 1536
H = 12
KV = 2
HD = 128
STEP = 10


EPS = 1e-06
THETA = 1000000.0
BETA_ONE = 0.9
BETA_TWO = 0.999
ADAM_EPS = 1e-08
CLIP = 1.0
NEG_BIG = -1e30
RATES = (0.03, 0.03, 0.03, 0.8, 0.03, 0.03, 0.015, 0.8)
DECAYS = (0.1, 0.1, 0.1, 0.1, 0.1, 0.1, 0.1, 0.0)


def round_trip(values):
    return lax.optimization_barrier(values.astype(jnp.bfloat16)).astype(jnp.float32)


def rope_tables(pos_rows, head_dim):
    half_dim = head_dim // 2
    frequency = THETA ** (-(jnp.arange(half_dim, dtype=jnp.float32) * 2.0 / head_dim))
    angles = pos_rows.astype(jnp.float32)[:, None] * frequency[None, :]
    cosine = jnp.cos(angles)
    sine_part = jnp.sin(angles)
    return (jnp.concatenate([cosine, cosine], -1), jnp.concatenate([sine_part, sine_part], -1))


def rotate(values, cosine, sine_part):
    half_dim = values.shape[-1] // 2
    turned = jnp.concatenate([-values[..., half_dim:], values[..., :half_dim]], -1)
    return values * cosine[:, None, :] + turned * sine_part[:, None, :]


def rotate_back(gradient, cosine, sine_part):
    half_dim = gradient.shape[-1] // 2
    scaled = gradient * sine_part[:, None, :]
    return gradient * cosine[:, None, :] + jnp.concatenate(
        [scaled[..., half_dim:], -scaled[..., :half_dim]], -1
    )


def norm_forward(rows_in):
    inverse = lax.rsqrt(jnp.mean(rows_in * rows_in, -1, keepdims=True) + EPS)
    return (rows_in * inverse, inverse)


def norm_backward(upstream, normed, inverse, gains):
    scaled = upstream * gains
    inner = jnp.mean(scaled * normed, -1, keepdims=True)
    return (inverse * (scaled - normed * inner), jnp.sum(upstream * normed, 0))


def contract_rows(left, right):
    return lax.dot_general(
        left, right, (((0,), (0,)), ((), ())), preferred_element_type=jnp.float32
    )


def contract_cols(left, right):
    return lax.dot_general(
        left, right, (((1,), (1,)), ((), ())), preferred_element_type=jnp.float32
    )


def visible(query_seg, query_pos, key_seg, key_pos):
    same_doc = (query_seg[:, None] == key_seg[None, :]) & (key_pos[None, :] <= query_pos[:, None])
    prompt_keys = (key_seg[None, :] == 0) & (query_seg[:, None] != 0)
    return same_doc | prompt_keys


def attend_forward(queries, key_all, value_all, query_seg, query_pos, key_seg, key_pos):
    row_count, heads_dev, head_dim = queries.shape
    key_total = key_all.shape[0]
    block_len = math.gcd(key_total, 1024)
    score_scale = head_dim ** (-0.5)

    def step(state_now, block_index):
        start = block_index * block_len
        key_blk = lax.dynamic_slice_in_dim(key_all, start, block_len, 0)
        value_blk = lax.dynamic_slice_in_dim(value_all, start, block_len, 0)
        allowed = visible(
            query_seg,
            query_pos,
            lax.dynamic_slice_in_dim(key_seg, start, block_len),
            lax.dynamic_slice_in_dim(key_pos, start, block_len),
        )[:, None, :]

        def compute(state_in):
            row_top, row_mass, accumulated = state_in
            scores = (
                jnp.einsum("rhd,kd->rhk", queries, key_blk, preferred_element_type=jnp.float32)
                * score_scale
            )
            scores = jnp.where(allowed, scores, NEG_BIG)
            new_top = jnp.maximum(row_top, jnp.max(scores, -1))
            weights = jnp.where(allowed, jnp.exp(scores - new_top[..., None]), 0.0)
            shrink = jnp.exp(row_top - new_top)
            row_mass = row_mass * shrink + jnp.sum(weights, -1)
            accumulated = accumulated * shrink[..., None] + jnp.einsum(
                "rhk,kd->rhd",
                weights.astype(jnp.bfloat16),
                value_blk,
                preferred_element_type=jnp.float32,
            )
            return (new_top, row_mass, accumulated)

        state_next = compute(state_now)
        return (state_next, None)

    initial = (
        jnp.full((row_count, heads_dev), NEG_BIG, jnp.float32),
        jnp.zeros((row_count, heads_dev), jnp.float32),
        jnp.zeros((row_count, heads_dev, head_dim), jnp.float32),
    )
    (row_top, row_mass, accumulated), _ = lax.scan(
        step, initial, jnp.arange(key_total // block_len)
    )
    return (accumulated / row_mass[..., None], row_top + jnp.log(row_mass))


def attend_backward(
    queries,
    key_all,
    value_all,
    out_heads,
    log_mass,
    row_delta,
    query_seg,
    query_pos,
    key_seg,
    key_pos,
):
    row_count, heads_dev, head_dim = queries.shape
    key_total = key_all.shape[0]
    block_len = math.gcd(key_total, 1024)
    score_scale = head_dim ** (-0.5)

    def step(query_acc, block_index):
        start = block_index * block_len
        key_blk = lax.dynamic_slice_in_dim(key_all, start, block_len, 0)
        value_blk = lax.dynamic_slice_in_dim(value_all, start, block_len, 0)
        allowed = visible(
            query_seg,
            query_pos,
            lax.dynamic_slice_in_dim(key_seg, start, block_len),
            lax.dynamic_slice_in_dim(key_pos, start, block_len),
        )[:, None, :]

        def compute(acc_in):
            scores = (
                jnp.einsum("rhd,kd->rhk", queries, key_blk, preferred_element_type=jnp.float32)
                * score_scale
            )
            weights = jnp.where(allowed, jnp.exp(scores - log_mass[..., None]), 0.0)
            value_grad = jnp.einsum(
                "rhk,rhd->kd",
                weights.astype(jnp.bfloat16),
                out_heads,
                preferred_element_type=jnp.float32,
            )
            weight_grad = jnp.einsum(
                "rhd,kd->rhk", out_heads, value_blk, preferred_element_type=jnp.float32
            )
            score_grad = (weights * (weight_grad - row_delta[..., None])).astype(jnp.bfloat16)
            acc_out = acc_in + jnp.einsum(
                "rhk,kd->rhd", score_grad, key_blk, preferred_element_type=jnp.float32
            )
            key_grad = jnp.einsum(
                "rhk,rhd->kd", score_grad, queries, preferred_element_type=jnp.float32
            )
            return (acc_out, key_grad, value_grad)

        acc_next, key_grad, value_grad = compute(query_acc)
        return (acc_next, (key_grad, value_grad))

    query_grad, (key_blocks, value_blocks) = lax.scan(
        step,
        jnp.zeros((row_count, heads_dev, head_dim), jnp.float32),
        jnp.arange(key_total // block_len),
    )
    return (
        query_grad * score_scale,
        key_blocks.reshape(key_total, head_dim) * score_scale,
        value_blocks.reshape(key_total, head_dim),
    )


def gather_ffn(gate_master, up_master, down_master):
    return (
        lax.all_gather(gate_master.astype(jnp.bfloat16), "blk", axis=0, tiled=True),
        lax.all_gather(up_master.astype(jnp.bfloat16), "blk", axis=0, tiled=True),
        lax.all_gather(down_master.astype(jnp.bfloat16), "blk", axis=1, tiled=True),
    )


def gather_keys(key_heads, value_heads):
    return (
        lax.all_gather(key_heads, "blk", axis=0, tiled=True),
        lax.all_gather(value_heads, "blk", axis=0, tiled=True),
    )


def adam_update(master, first, second, gradient, factor, rate, decay):
    clipped = gradient * factor
    first_new = BETA_ONE * first + (1.0 - BETA_ONE) * clipped
    second_new = BETA_TWO * second + (1.0 - BETA_TWO) * clipped * clipped
    first_hat = first_new / (1.0 - BETA_ONE**STEP)
    second_hat = second_new / (1.0 - BETA_TWO**STEP)
    master_new = master - rate * (first_hat / (jnp.sqrt(second_hat) + ADAM_EPS) + decay * master)
    return (master_new, first_new, second_new, master_new.astype(jnp.bfloat16))


def body(
    hidden_in,
    out_grad,
    segments,
    positions,
    query_master,
    query_first,
    query_second,
    key_master,
    key_first,
    key_second,
    value_master,
    value_first,
    value_second,
    output_master,
    output_first,
    output_second,
    gate_master,
    gate_first,
    gate_second,
    up_master,
    up_first,
    up_second,
    down_master,
    down_first,
    down_second,
    small_master,
    small_first,
    small_second,
):
    ulysses_size = lax.axis_size("ulysses")
    cycle_size = lax.axis_size("blk")
    ulysses_id = lax.axis_index("ulysses")
    cycle_id = lax.axis_index("blk")
    tok_rows = hidden_in.shape[0]
    query_width = H * HD
    kv_width = KV * HD
    heads_dev = H // ulysses_size
    repeat_by = ulysses_size // KV
    w_query, w_key, w_value, w_output, small_all = (
        lax.all_gather(query_master.astype(jnp.bfloat16), ("ulysses", "blk"), axis=0, tiled=True),
        lax.all_gather(key_master.astype(jnp.bfloat16), ("ulysses", "blk"), axis=0, tiled=True),
        lax.all_gather(value_master.astype(jnp.bfloat16), ("ulysses", "blk"), axis=0, tiled=True),
        lax.all_gather(output_master.astype(jnp.bfloat16), ("ulysses", "blk"), axis=1, tiled=True),
        lax.all_gather(small_master.astype(jnp.bfloat16), ("ulysses", "blk"), axis=0, tiled=True),
    )
    small_vals = small_all.astype(jnp.float32).reshape(kv_width, -1).T.reshape(-1)
    bias_query = small_vals[:query_width]
    bias_key = small_vals[query_width : query_width + kv_width]
    bias_value = small_vals[query_width + kv_width : query_width + 2 * kv_width]
    gain_one = small_vals[query_width + 2 * kv_width : query_width + 2 * kv_width + D]
    gain_two = small_vals[query_width + 2 * kv_width + D :]
    ffn_gate, ffn_up, ffn_down = gather_ffn(gate_master, up_master, down_master)
    seg_grid = segments.reshape(ulysses_size, cycle_size, tok_rows)
    pos_grid = positions.reshape(ulysses_size, cycle_size, tok_rows)
    own_start = (ulysses_id * cycle_size + cycle_id) * tok_rows
    own_pos = lax.dynamic_slice_in_dim(positions, own_start, tok_rows)
    query_seg = lax.dynamic_index_in_dim(seg_grid, cycle_id, 1, keepdims=False).reshape(-1)
    query_pos = lax.dynamic_index_in_dim(pos_grid, cycle_id, 1, keepdims=False).reshape(-1)
    key_seg = jnp.transpose(seg_grid, (1, 0, 2)).reshape(-1)
    key_pos = jnp.transpose(pos_grid, (1, 0, 2)).reshape(-1)
    hidden = hidden_in.astype(jnp.float32)
    normed_one, inverse_one = norm_forward(hidden)
    attn_input = (normed_one * gain_one).astype(jnp.bfloat16)
    query_pre = jnp.dot(attn_input, w_query, preferred_element_type=jnp.float32) + bias_query
    key_pre = jnp.dot(attn_input, w_key, preferred_element_type=jnp.float32) + bias_key
    value_pre = jnp.dot(attn_input, w_value, preferred_element_type=jnp.float32) + bias_value
    cosine, sine_part = rope_tables(own_pos, HD)
    query_send = (
        rotate(query_pre.reshape(tok_rows, H, HD), cosine, sine_part)
        .reshape(tok_rows, query_width)
        .astype(jnp.bfloat16)
    )
    key_rot = rotate(key_pre.reshape(tok_rows, KV, HD), cosine, sine_part)
    key_send = (
        jnp.repeat(key_rot, repeat_by, axis=1)
        .reshape(tok_rows, ulysses_size * HD)
        .astype(jnp.bfloat16)
    )
    value_send = (
        jnp.repeat(value_pre.reshape(tok_rows, KV, HD), repeat_by, axis=1)
        .reshape(tok_rows, ulysses_size * HD)
        .astype(jnp.bfloat16)
    )
    query_heads, key_heads, value_heads = (
        lax.all_to_all(query_send, "ulysses", split_axis=1, concat_axis=0, tiled=True),
        lax.all_to_all(key_send, "ulysses", split_axis=1, concat_axis=0, tiled=True),
        lax.all_to_all(value_send, "ulysses", split_axis=1, concat_axis=0, tiled=True),
    )
    row_count = query_heads.shape[0]
    queries = query_heads.reshape(row_count, heads_dev, HD)
    key_all, value_all = gather_keys(key_heads, value_heads)
    attended, log_mass = attend_forward(
        queries, key_all, value_all, query_seg, query_pos, key_seg, key_pos
    )
    out_send = attended.reshape(row_count, heads_dev * HD).astype(jnp.bfloat16)
    attn_tok = lax.all_to_all(out_send, "ulysses", split_axis=0, concat_axis=1, tiled=True)
    residual = hidden + jnp.dot(attn_tok, w_output, preferred_element_type=jnp.float32)
    normed_two, inverse_two = norm_forward(residual)
    ffn_input = (normed_two * gain_two).astype(jnp.bfloat16)
    ffn_all, grad_all = (
        lax.all_gather(ffn_input, "ulysses", axis=0, tiled=True),
        lax.all_gather(out_grad, "ulysses", axis=0, tiled=True),
    )
    gate_value = jnp.dot(ffn_all, ffn_gate, preferred_element_type=jnp.float32)
    up_value = jnp.dot(ffn_all, ffn_up, preferred_element_type=jnp.float32)
    sigmoid_gate = jax.nn.sigmoid(gate_value)
    silu_gate = gate_value * sigmoid_gate
    activation = (silu_gate * up_value).astype(jnp.bfloat16)
    ffn_part = jnp.dot(activation, ffn_down, preferred_element_type=jnp.float32)
    ffn_out = lax.psum_scatter(
        ffn_part.astype(jnp.bfloat16), "ulysses", scatter_dimension=0, tiled=True
    ).astype(jnp.float32)
    mixed = (residual + ffn_out).astype(jnp.bfloat16)
    down_grad = contract_rows(activation, grad_all)
    act_grad = contract_cols(grad_all, ffn_down)
    gate_grad = (
        act_grad * up_value * sigmoid_gate * (1.0 + gate_value * (1.0 - sigmoid_gate))
    ).astype(jnp.bfloat16)
    up_grad = (act_grad * silu_gate).astype(jnp.bfloat16)
    gate_w_grad = contract_rows(ffn_all, gate_grad)
    up_w_grad = contract_rows(ffn_all, up_grad)
    ffn_in_part = contract_cols(gate_grad, ffn_gate) + contract_cols(up_grad, ffn_up)
    g_gate, g_up, g_down = (
        lax.psum_scatter(
            gate_w_grad.astype(jnp.bfloat16), "blk", scatter_dimension=0, tiled=True
        ).astype(jnp.float32),
        lax.psum_scatter(
            up_w_grad.astype(jnp.bfloat16), "blk", scatter_dimension=0, tiled=True
        ).astype(jnp.float32),
        lax.psum_scatter(
            down_grad.astype(jnp.bfloat16), "blk", scatter_dimension=1, tiled=True
        ).astype(jnp.float32),
    )
    ffn_in_grad = lax.psum_scatter(
        ffn_in_part.astype(jnp.bfloat16), "ulysses", scatter_dimension=0, tiled=True
    ).astype(jnp.float32)
    norm_two_grad, gain_two_grad = norm_backward(ffn_in_grad, normed_two, inverse_two, gain_two)
    residual_grad = out_grad.astype(jnp.float32) + norm_two_grad
    branch_grad = residual_grad.astype(jnp.bfloat16)
    output_w_grad = contract_rows(attn_tok, branch_grad)
    attn_tok_grad = contract_cols(branch_grad, w_output).astype(jnp.bfloat16)
    out_heads = lax.all_to_all(
        attn_tok_grad, "ulysses", split_axis=1, concat_axis=0, tiled=True
    ).reshape(row_count, heads_dev, HD)
    row_delta = jnp.sum(out_heads.astype(jnp.float32) * attended, -1)
    query_grad, key_grad_all, value_grad_all = attend_backward(
        queries,
        key_all,
        value_all,
        out_heads,
        log_mass,
        row_delta,
        query_seg,
        query_pos,
        key_seg,
        key_pos,
    )
    key_grad_own, value_grad_own = (
        lax.psum_scatter(
            key_grad_all.astype(jnp.bfloat16), "blk", scatter_dimension=0, tiled=True
        ).astype(jnp.float32),
        lax.psum_scatter(
            value_grad_all.astype(jnp.bfloat16), "blk", scatter_dimension=0, tiled=True
        ).astype(jnp.float32),
    )
    query_grad_tok, key_grad_tok, value_grad_tok = (
        lax.all_to_all(
            query_grad.reshape(row_count, heads_dev * HD).astype(jnp.bfloat16),
            "ulysses",
            split_axis=0,
            concat_axis=1,
            tiled=True,
        ).astype(jnp.float32),
        lax.all_to_all(
            key_grad_own.astype(jnp.bfloat16), "ulysses", split_axis=0, concat_axis=1, tiled=True
        ).astype(key_grad_own.dtype),
        lax.all_to_all(
            value_grad_own.astype(jnp.bfloat16), "ulysses", split_axis=0, concat_axis=1, tiled=True
        ).astype(value_grad_own.dtype),
    )
    query_rot_grad = round_trip(query_grad_tok.reshape(tok_rows, H, HD))
    key_rot_grad = round_trip(jnp.sum(key_grad_tok.reshape(tok_rows, KV, repeat_by, HD), 2))
    query_pre_grad = (
        rotate_back(query_rot_grad, cosine, sine_part)
        .reshape(tok_rows, query_width)
        .astype(jnp.bfloat16)
    )
    key_pre_grad = (
        rotate_back(key_rot_grad, cosine, sine_part)
        .reshape(tok_rows, kv_width)
        .astype(jnp.bfloat16)
    )
    value_pre_grad = (
        jnp.sum(value_grad_tok.reshape(tok_rows, KV, repeat_by, HD), 2)
        .reshape(tok_rows, kv_width)
        .astype(jnp.bfloat16)
    )
    bias_query_grad = jnp.sum(query_pre_grad, 0, dtype=jnp.float32)
    bias_key_grad = jnp.sum(key_pre_grad, 0, dtype=jnp.float32)
    bias_value_grad = jnp.sum(value_pre_grad, 0, dtype=jnp.float32)
    query_w_grad = contract_rows(attn_input, query_pre_grad)
    key_w_grad = contract_rows(attn_input, key_pre_grad)
    value_w_grad = contract_rows(attn_input, value_pre_grad)
    attn_in_grad = (
        contract_cols(query_pre_grad, w_query)
        + contract_cols(key_pre_grad, w_key)
        + contract_cols(value_pre_grad, w_value)
    )
    norm_one_grad, gain_one_grad = norm_backward(attn_in_grad, normed_one, inverse_one, gain_one)
    input_grad = residual_grad + norm_one_grad
    small_ordered = jnp.concatenate(
        [bias_query_grad, bias_key_grad, bias_value_grad, gain_one_grad, gain_two_grad]
    )
    small_grad = small_ordered.reshape(-1, kv_width).T.reshape(-1)
    g_query, g_key, g_value, g_output, g_small = (
        lax.psum_scatter(query_w_grad, ("ulysses", "blk"), scatter_dimension=0, tiled=True),
        lax.psum_scatter(key_w_grad, ("ulysses", "blk"), scatter_dimension=0, tiled=True),
        lax.psum_scatter(value_w_grad, ("ulysses", "blk"), scatter_dimension=0, tiled=True),
        lax.psum_scatter(output_w_grad, ("ulysses", "blk"), scatter_dimension=1, tiled=True),
        lax.psum_scatter(small_grad, ("ulysses", "blk"), scatter_dimension=0, tiled=True),
    )
    shards = (g_query, g_key, g_value, g_output, g_gate, g_up, g_down, g_small)
    local_squares = jnp.float32(0.0)
    for shard_grad in shards:
        local_squares = local_squares + jnp.sum(shard_grad * shard_grad)
    total_squares = lax.psum(local_squares, ("ulysses", "blk"))
    grad_norm = jnp.sqrt(total_squares)
    factor = CLIP / jnp.maximum(grad_norm, CLIP)
    masters = (
        query_master,
        key_master,
        value_master,
        output_master,
        gate_master,
        up_master,
        down_master,
        small_master,
    )
    firsts = (
        query_first,
        key_first,
        value_first,
        output_first,
        gate_first,
        up_first,
        down_first,
        small_first,
    )
    seconds = (
        query_second,
        key_second,
        value_second,
        output_second,
        gate_second,
        up_second,
        down_second,
        small_second,
    )
    updates = [
        adam_update(
            masters[slot],
            firsts[slot],
            seconds[slot],
            shards[slot],
            factor,
            RATES[slot],
            DECAYS[slot],
        )
        for slot in range(8)
    ]
    return (
        mixed,
        input_grad,
        grad_norm,
        updates[0][0],
        updates[0][1],
        updates[0][2],
        updates[0][3],
        updates[1][0],
        updates[1][1],
        updates[1][2],
        updates[1][3],
        updates[2][0],
        updates[2][1],
        updates[2][2],
        updates[2][3],
        updates[3][0],
        updates[3][1],
        updates[3][2],
        updates[3][3],
        updates[4][0],
        updates[4][1],
        updates[4][2],
        updates[4][3],
        updates[5][0],
        updates[5][1],
        updates[5][2],
        updates[5][3],
        updates[6][0],
        updates[6][1],
        updates[6][2],
        updates[6][3],
        updates[7][0],
        updates[7][1],
        updates[7][2],
        updates[7][3],
    )


def solution(mesh):
    in_specs = (
        P(("ulysses", "blk"), None),
        P(("ulysses", "blk"), None),
        P(),
        P(),
        P(("ulysses", "blk"), None),
        P(("ulysses", "blk"), None),
        P(("ulysses", "blk"), None),
        P(("ulysses", "blk"), None),
        P(("ulysses", "blk"), None),
        P(("ulysses", "blk"), None),
        P(("ulysses", "blk"), None),
        P(("ulysses", "blk"), None),
        P(("ulysses", "blk"), None),
        P(None, ("ulysses", "blk")),
        P(None, ("ulysses", "blk")),
        P(None, ("ulysses", "blk")),
        P("blk", "ulysses"),
        P("blk", "ulysses"),
        P("blk", "ulysses"),
        P("blk", "ulysses"),
        P("blk", "ulysses"),
        P("blk", "ulysses"),
        P("ulysses", "blk"),
        P("ulysses", "blk"),
        P("ulysses", "blk"),
        P(("ulysses", "blk")),
        P(("ulysses", "blk")),
        P(("ulysses", "blk")),
    )
    out_specs = (
        P(("ulysses", "blk"), None),
        P(("ulysses", "blk"), None),
        P(),
        P(("ulysses", "blk"), None),
        P(("ulysses", "blk"), None),
        P(("ulysses", "blk"), None),
        P(("ulysses", "blk"), None),
        P(("ulysses", "blk"), None),
        P(("ulysses", "blk"), None),
        P(("ulysses", "blk"), None),
        P(("ulysses", "blk"), None),
        P(("ulysses", "blk"), None),
        P(("ulysses", "blk"), None),
        P(("ulysses", "blk"), None),
        P(("ulysses", "blk"), None),
        P(None, ("ulysses", "blk")),
        P(None, ("ulysses", "blk")),
        P(None, ("ulysses", "blk")),
        P(None, ("ulysses", "blk")),
        P("blk", "ulysses"),
        P("blk", "ulysses"),
        P("blk", "ulysses"),
        P("blk", "ulysses"),
        P("blk", "ulysses"),
        P("blk", "ulysses"),
        P("blk", "ulysses"),
        P("blk", "ulysses"),
        P("ulysses", "blk"),
        P("ulysses", "blk"),
        P("ulysses", "blk"),
        P("ulysses", "blk"),
        P(("ulysses", "blk")),
        P(("ulysses", "blk")),
        P(("ulysses", "blk")),
        P(("ulysses", "blk")),
    )
    return jax.shard_map(body, mesh=mesh, in_specs=in_specs, out_specs=out_specs, check_vma=False)
```

profile of v0, /device:TPU:0, one launch (start us, length us, event | category | flops | bytes accessed | tf_op | source)
XLA Modules:
  0.0 1951.1 jit_solution(12406316158313001888)
XLA Ops:
  9.9 43.1 %all-reduce = bf16[5120]{0:T(1024)(128)(2,1)S(1)} all-reduce(bf16[5120]{0:T(1024)(128)(2,1)S(1)} %dynamic-update-slice), channel_id=1, replica_groups=mesh['ulysses'=4,'blk'=8] {'ulysses','blk'}, use_global_device_ids=true, to_apply=%add | all-reduce | flops 5120 | bytes 20480
  55.3 71.5 %all_gather.37 = bf16[1536,256]{1,0:T(8,128)(2,1)S(1)} all-gather(bf16[48,256]{1,0:T(8,128)(2,1)S(1)} %convert_element_type.234), channel_id=1, replica_groups=mesh['ulysses'=4,'blk'=8] {'ulysses','blk'}, dimensions={0}, use_global_device_ids=true | all-gather | bytes 811008 | tf_op jit(solution)/shard_map/all_gather | solution.py:265
  136.6 69.2 %all_gather.40 = bf16[1536,256]{1,0:T(8,128)(2,1)S(1)} all-gather(bf16[48,256]{1,0:T(8,128)(2,1)S(1)} %convert_element_type.240), channel_id=1, replica_groups=mesh['ulysses'=4,'blk'=8] {'ulysses','blk'}, dimensions={0}, use_global_device_ids=true | all-gather | bytes 811008 | tf_op jit(solution)/shard_map/all_gather | solution.py:266
  236.2 16.5 all-gather.14.cloned.1.call-done
  252.7 60.1 %while.30 = (s32[]{:T(128)}, f32[512,3]{0,1:T(4,128)S(1)}, f32[512,3]{0,1:T(4,128)S(1)}, f32[512,3,128]{2,0,1:T(8,128)S(1)}, s32[4,128]{1,0:T(4,128)S(1)}, /*ind...) while((s32[]{:T(128)}, f32[512,3]{0,1:T(4,128)S(1)}, ...), condition=%wide.region_4.5_spmd.clone, body=%wide.region_1.4_spmd.clone.sunk | while | flops 828974080 | bytes 48760068 | solution.py:126
  338.6 90.1 %all-gather.20.cloned.1.call-done = bf16[1536,2240]{1,0:T(8,128)(2,1)} async-done(((bf16[192,2240]{1,0:T(8,128)(2,1)}), bf16[1536,2240]{1,0:T(8,128)(2,1)}) %all-gather.20.cloned.1.call-update) | async-done | bytes 6881296 | tf_op jit(solution)/shard_map/all_gather | solution.py:201
  428.8 19.9 %all-gather.18.cloned.1.call-done = bf16[512,1536]{1,0:T(8,128)(2,1)} async-done(((bf16[128,1536]{1,0:T(8,128)(2,1)}), bf16[512,1536]{1,0:T(8,128)(2,1)}) %all-gather.18.cloned.1.call-update) | async-done | bytes 1572880 | tf_op jit(solution)/shard_map/all_gather | solution.py:325
  448.6 9.4 fusion.126
  458.1 102.2 %all-gather.22.cloned.1.call-done = bf16[1536,2240]{1,0:T(8,128)(2,1)} async-done(((bf16[192,2240]{1,0:T(8,128)(2,1)}), bf16[1536,2240]{1,0:T(8,128)(2,1)}) %all-gather.22.cloned.1.call-update) | async-done | bytes 6881296 | tf_op jit(solution)/shard_map/all_gather | solution.py:202
  560.2 9.3 fusion.127
  569.5 10.1 all-gather.26.cloned.1.call-done
  579.6 111.6 %all-gather.24.cloned.1.call-done = bf16[2240,1536]{0,1:T(8,128)(2,1)} async-done(((bf16[2240,192]{0,1:T(8,128)(2,1)}), bf16[2240,1536]{0,1:T(8,128)(2,1)}) %all-gather.24.cloned.1.call-update) | async-done | bytes 6881296 | tf_op jit(solution)/shard_map/all_gather | solution.py:203
  691.3 13.6 multiply_convert_fusion
  717.8 8.8 convolution_convert_fusion.3
  726.6 17.7 reduce-scatter.14.cloned.1.call-done
  745.6 30.2 %reduce-scatter.12.cloned.1.call-done = bf16[128,1536]{1,0:T(8,128)(2,1)} async-done(((bf16[512,1536]{1,0:T(8,128)(2,1)}), bf16[128,1536]{1,0:T(8,128)(2,1)}) %reduce-scatter.12.cloned.1.call-update) | async-done | bytes 393232 | tf_op jit(solution)/shard_map/reduce_scatter | solution.py:334
  795.3 65.1 %while.31 = (s32[]{:T(128)}, f32[512,3,128]{2,0,1:T(8,128)}, f32[4,1024,128]{2,1,0:T(8,128)}, bf16[4,1024,128]{2,1,0:T(8,128)(2,1)}, s32[4,128]{1,0:T(4,128)S(1)...) while((s32[]{:T(128)}, f32[512,3,128]{2,0,1:T(8,128)}, ...), condition=%wide.region_11.12_spmd.clone, body=%wide.region_10.11_spmd.clone.sunk | while | flops 2032010752 | bytes 89256712 | solution.py:187
  864.0 62.7 %reduce-scatter.16.cloned.1.call-done = bf16[512,128]{1,0:T(8,128)(2,1)} async-done(((bf16[4096,128]{1,0:T(8,128)(2,1)}), bf16[512,128]{1,0:T(8,128)(2,1)}) %reduce-scatter.16.cloned.1.call-update) | async-done | bytes 131088 | tf_op jit(solution)/shard_map/reduce_scatter | solution.py:383
  926.8 7.9 all_to_all.130
  936.8 56.8 %reduce-scatter.18.cloned.1.call-done = bf16[512,128]{1,0:T(8,128)(2,1)} async-done(((bf16[4096,128]{1,0:T(8,128)(2,1)}), bf16[512,128]{1,0:T(8,128)(2,1)}) %reduce-scatter.18.cloned.1.call-update) | async-done | bytes 131088 | tf_op jit(solution)/shard_map/reduce_scatter | solution.py:386
  1003.6 9.0 convolution_convert_fusion.2
  1012.6 8.9 convolution_convert_fusion.1
  1021.6 8.8 convolution_convert_fusion
  1038.4 9.9 all_to_all.132
  1060.0 39.3 %all-reduce.1 = f32[5120]{0:T(1024)S(1)} all-reduce(f32[5120]{0:T(1024)S(1)} %reshape.406), channel_id=13, replica_groups=mesh['ulysses'=4,'blk'=8] {'ulysses','blk'}, use_global_device_ids=true, to_apply=%region_36.37.clone | all-reduce | flops 5120 | bytes 40960
  1101.4 95.7 %reduce-scatter.24.cloned.1.call-done = f32[48,256]{1,0:T(8,128)} async-done(((f32[1536,256]{1,0:T(8,128)}), f32[48,256]{1,0:T(8,128)}) %reduce-scatter.24.cloned.1.call-update) | async-done | bytes 49168 | tf_op jit(solution)/shard_map/reduce_scatter | solution.py:442
  1198.5 130.2 %reduce-scatter.28.cloned.1.call-done = bf16[192,2240]{1,0:T(8,128)(2,1)} async-done(((bf16[1536,2240]{1,0:T(8,128)(2,1)}), bf16[192,2240]{1,0:T(8,128)(2,1)}) %reduce-scatter.28.cloned.1.call-update) | async-done | bytes 860176 | tf_op jit(solution)/shard_map/reduce_scatter | solution.py:348
  1330.9 129.8 %reduce-scatter.30.cloned.1.call-done = bf16[192,2240]{1,0:T(8,128)(2,1)} async-done(((bf16[1536,2240]{1,0:T(8,128)(2,1)}), bf16[192,2240]{1,0:T(8,128)(2,1)}) %reduce-scatter.30.cloned.1.call-update) | async-done | bytes 860176 | tf_op jit(solution)/shard_map/reduce_scatter | solution.py:351
  1463.0 129.4 %reduce-scatter.32.cloned.1.call-done = bf16[2240,192]{0,1:T(8,128)(2,1)} async-done(((bf16[2240,1536]{0,1:T(8,128)(2,1)}), bf16[2240,192]{0,1:T(8,128)(2,1)}) %reduce-scatter.32.cloned.1.call-update) | async-done | bytes 860176 | tf_op jit(solution)/shard_map/reduce_scatter | solution.py:354
  1594.7 139.2 %reduce-scatter.26.cloned.1.call-done = f32[1536,48]{0,1:T(8,128)} async-done(((f32[1536,1536]{0,1:T(8,128)}), f32[1536,48]{0,1:T(8,128)}) %reduce-scatter.26.cloned.1.call-update) | async-done | bytes 294928 | tf_op jit(solution)/shard_map/reduce_scatter | solution.py:443
  1735.5 138.8 %reduce-scatter.20.cloned.1.call-done = f32[48,1536]{1,0:T(8,128)} async-done(((f32[1536,1536]{1,0:T(8,128)}), f32[48,1536]{1,0:T(8,128)}) %reduce-scatter.20.cloned.1.call-update) | async-done | bytes 294928 | tf_op jit(solution)/shard_map/reduce_scatter | solution.py:440
  1882.3 40.1 %psum.7 = f32[]{:T(128)} all-reduce(f32[]{:T(128)S(6)} %add.316), channel_id=1, replica_groups=mesh['ulysses'=4,'blk'=8] {'ulysses','blk'}, use_global_device_ids=true, to_apply=%region_38.39 | all-reduce | flops 1 | bytes 8 | tf_op jit(solution)/shard_map/psum | solution.py:450
  (500 shorter events, 292.1 us)
Async XLA Ops:
  7.2 209.9 %all-gather.12.cloned.1.call-start = ((), (), s32[]{:S(2)}) async-start(), calls=%async_computation.20 | async-start | bytes 4866048 | tf_op jit(solution)/shard_map/all_gather | solution.py:264
  9.0 227.2 %all-gather.10.cloned.1.call-start = ((), (), s32[]{:S(2)}) async-start(), calls=%async_computation.19 | async-start | bytes 1179648 | tf_op jit(solution)/shard_map/all_gather | solution.py:209
  54.0 163.1 %copy-start.40 = (f32[1536]{0:T(1024)}, f32[1536]{0:T(1024)S(1)}, u32[]{:S(2)}) copy-start(f32[1536]{0:T(1024)S(1)} %mul.545) | copy-start | bytes 18436
  55.3 161.9 %copy-start.61 = (f32[128]{0:T(128)}, f32[128]{0:T(128)S(1)}, u32[]{:S(2)}) copy-start(f32[128]{0:T(128)S(1)} %add_rsqrt_fusion.1) | copy-start | bytes 1540
  128.6 87.0 %copy-start.33 = (f32[128,128]{1,0:T(8,128)}, f32[128,128]{1,0:T(8,128)S(1)}, u32[]{:S(2)}) copy-start(f32[128,128]{1,0:T(8,128)S(1)} %get-tuple-element.507) | copy-start | bytes 196612
  128.6 87.1 %copy-start.31 = (f32[128,128]{1,0:T(8,128)}, f32[128,128]{1,0:T(8,128)S(1)}, u32[]{:S(2)}) copy-start(f32[128,128]{1,0:T(8,128)S(1)} %get-tuple-element.506) | copy-start | bytes 196612
  128.7 86.2 %copy-start.26 = (f32[1536,48]{0,1:T(8,128)S(1)}, f32[1536,48]{0,1:T(8,128)}, u32[]{:S(2)}) copy-start(f32[1536,48]{0,1:T(8,128)} %param.45) | copy-start | bytes 884740
  136.6 116.1 %all-gather.14.cloned.1.call-start = ((), (), s32[]{:S(2)}) async-start(), calls=%async_computation.21 | async-start | bytes 1179648 | tf_op jit(solution)/shard_map/all_gather | solution.py:210
  214.8 104.9 %all-gather.16.cloned.1.call-start = ((), (), s32[]{:S(2)}) async-start(), calls=%async_computation.22 | async-start | bytes 4866048 | tf_op jit(solution)/shard_map/all_gather | solution.py:267
  224.4 11.0 all-to-all-start.1
  228.0 200.7 %all-gather.20.cloned.1.call-start = ((), (), s32[]{:S(2)}) async-start(), calls=%async_computation.24 | async-start | bytes 7962624 | tf_op jit(solution)/shard_map/all_gather | solution.py:201
  316.1 10.9 all-to-all-start.3
  319.5 129.1 %all-gather.18.cloned.1.call-start = ((), (), s32[]{:S(2)}) async-start(), calls=%async_computation.23 | async-start | bytes 1966080 | tf_op jit(solution)/shard_map/all_gather | solution.py:325
  332.5 227.7 %all-gather.22.cloned.1.call-start = ((), (), s32[]{:S(2)}) async-start(), calls=%async_computation.25 | async-start | bytes 7962624 | tf_op jit(solution)/shard_map/all_gather | solution.py:202
  335.0 244.6 %all-gather.26.cloned.1.call-start = ((), (), s32[]{:S(2)}) async-start(), calls=%async_computation.28 | async-start | bytes 1966080 | tf_op jit(solution)/shard_map/all_gather | solution.py:326
  335.8 355.5 %all-gather.24.cloned.1.call-start = ((), (), s32[]{:S(2)}) async-start(), calls=%async_computation.26 | async-start | bytes 7962624 | tf_op jit(solution)/shard_map/all_gather | solution.py:203
  338.4 405.9 %reduce-scatter.14.cloned.1.call-start = ((), (), s32[]{:S(2)}) async-start(), calls=%async_computation.29 | async-start | bytes 1966080 | tf_op jit(solution)/shard_map/reduce_scatter | solution.py:358
  717.8 58.0 %reduce-scatter.12.cloned.1.call-start = ((), (), s32[]{:S(2)}) async-start(), calls=%async_computation.27 | async-start | bytes 1966080 | tf_op jit(solution)/shard_map/reduce_scatter | solution.py:334
  782.3 10.9 all-to-all-start.4
  785.8 141.0 %reduce-scatter.16.cloned.1.call-start = ((), (), s32[]{:S(2)}) async-start(), calls=%async_computation.30 | async-start | bytes 1179648 | tf_op jit(solution)/shard_map/reduce_scatter | solution.py:383
  863.2 130.4 %reduce-scatter.18.cloned.1.call-start = ((), (), s32[]{:S(2)}) async-start(), calls=%async_computation.31 | async-start | bytes 1179648 | tf_op jit(solution)/shard_map/reduce_scatter | solution.py:386
  864.0 236.0 %reduce-scatter.22.cloned.1.call-start = ((), (), s32[]{:S(2)}) async-start(), calls=%async_computation.33 | async-start | bytes 1622016 | tf_op jit(solution)/shard_map/reduce_scatter | solution.py:441
  936.8 260.3 %reduce-scatter.24.cloned.1.call-start = ((), (), s32[]{:S(2)}) async-start(), calls=%async_computation.34 | async-start | bytes 1622016 | tf_op jit(solution)/shard_map/reduce_scatter | solution.py:442
  1003.3 325.4 %reduce-scatter.28.cloned.1.call-start = ((), (), s32[]{:S(2)}) async-start(), calls=%async_computation.36 | async-start | bytes 7962624 | tf_op jit(solution)/shard_map/reduce_scatter | solution.py:348
  1012.6 448.1 %reduce-scatter.30.cloned.1.call-start = ((), (), s32[]{:S(2)}) async-start(), calls=%async_computation.37 | async-start | bytes 7962624 | tf_op jit(solution)/shard_map/reduce_scatter | solution.py:351
  1021.6 570.8 %reduce-scatter.32.cloned.1.call-start = ((), (), s32[]{:S(2)}) async-start(), calls=%async_computation.38 | async-start | bytes 7962624 | tf_op jit(solution)/shard_map/reduce_scatter | solution.py:354
  1030.5 703.4 %reduce-scatter.26.cloned.1.call-start = ((), (), s32[]{:S(2)}) async-start(), calls=%async_computation.35 | async-start | bytes 9732096 | tf_op jit(solution)/shard_map/reduce_scatter | solution.py:443
  1036.8 837.5 %reduce-scatter.20.cloned.1.call-start = ((), (), s32[]{:S(2)}) async-start(), calls=%async_computation.32 | async-start | bytes 9732096 | tf_op jit(solution)/shard_map/reduce_scatter | solution.py:440
  1462.9 460.2 %copy-start.68 = (f32[160]{0:T(256)S(1)}, f32[160]{0:T(256)}, u32[]{:S(2)}) copy-start(f32[160]{0:T(256)} %param.57) | copy-start | bytes 1924
  1462.9 460.2 %copy-start.69 = (f32[160]{0:T(256)S(1)}, f32[160]{0:T(256)}, u32[]{:S(2)}) copy-start(f32[160]{0:T(256)} %param.58) | copy-start | bytes 1924
  1463.0 460.2 %copy-start.70 = (f32[160]{0:T(256)S(1)}, f32[160]{0:T(256)}, u32[]{:S(2)}) copy-start(f32[160]{0:T(256)} %param.59) | copy-start | bytes 1924
  1592.4 331.5 %copy-start.16 = (bf16[2240,192]{0,1:T(8,128)(2,1)S(1)}, bf16[2240,192]{0,1:T(8,128)(2,1)}, u32[]{:S(2)}) copy-start(bf16[2240,192]{0,1:T(8,128)(2,1)} %reduce-scatter.32.cloned.1.call-done) | copy-start | bytes 2580484
  (109 other events, 885.3 us)
Sparse Core Ops, SparseCore 0:
  11.5 69.1 all-gather.11
  136.7 38.5 all-gather.9
  214.9 37.6 all-gather.13
  256.0 62.4 all-gather.15
  321.1 107.6 all-gather.19
  430.7 17.8 all-gather.17
  451.4 108.7 all-gather.21
  561.8 17.8 all-gather.25
  582.4 108.7 all-gather.23
  717.9 26.3 reduce-scatter.13
  747.6 28.1 reduce-scatter.11
  863.3 63.3 reduce-scatter.15
  931.1 62.4 reduce-scatter.17
  999.3 96.0 reduce-scatter.21
  1101.0 96.0 reduce-scatter.23
  1200.6 128.0 reduce-scatter.27
  1332.6 128.0 reduce-scatter.29
  1464.3 128.0 reduce-scatter.31
  1599.3 134.5 reduce-scatter.25
  1739.6 134.6 reduce-scatter.19
where the time goes:
time: 1960 us; the launch traced here: 1950 us
  waiting for transfers between devices  1300 us (66%)
  blocking collectives  304 us (16%)
  matrix products  199 us (10%)
  other arithmetic  80.4 us (4%)
  local copies, waits for them, and re-layouts  23.7 us (1%)
  between operations  23 us (1%)
    reduce_scatter x1, waiting for transfers between devices, body(): lax.psum_scatter(output_w_grad, ('ulysses', 'blk'), scatter_dimension=1,...  139 us
    reduce_scatter x1, waiting for transfers between devices, body(): lax.psum_scatter(query_w_grad, ('ulysses', 'blk'), scatter_dimension=0, t...  139 us
    reduce_scatter x1, waiting for transfers between devices, body(): lax.psum_scatter(gate_w_grad.astype(jnp.bfloat16), 'blk', scatter_dimensi...  130 us
    reduce_scatter x1, waiting for transfers between devices, body(): lax.psum_scatter(up_w_grad.astype(jnp.bfloat16), 'blk', scatter_dimension...  130 us
    reduce_scatter x1, waiting for transfers between devices, body(): lax.psum_scatter(down_grad.astype(jnp.bfloat16), 'blk', scatter_dimension...  129 us
    all_gather x1, waiting for transfers between devices, gather_ffn(): lax.all_gather(down_master.astype(jnp.bfloat16), 'blk', axis=1, tiled=True)  112 us
    all_gather x1, waiting for transfers between devices, gather_ffn(): lax.all_gather(up_master.astype(jnp.bfloat16), 'blk', axis=0, tiled=True)  102 us
    reduce_scatter x1, waiting for transfers between devices, body(): lax.psum_scatter(value_w_grad, ('ulysses', 'blk'), scatter_dimension=0, t...  95.7 us
  transfers between devices with their start and end apart: 23, of which 19 were waited for; matrix products, arithmetic and copies ran while one was open for 9% of the time, Pallas kernels for 0%

commit v1 on v0

v1 whole, which is shorter than its diff:
```python
import functools
import math

import jax
import jax.numpy as jnp
from jax import lax
from jax.experimental import pallas as pl
from jax.experimental.pallas import tpu as pltpu
from jax.sharding import Mesh
from jax.sharding import PartitionSpec as P

D = 1536
H = 12
KV = 2
HD = 128
STEP = 10

EPS = 1e-06
THETA = 1000000.0
BETA_ONE = 0.9
BETA_TWO = 0.999
ADAM_EPS = 1e-08
CLIP = 1.0
NEG_BIG = -1e30
TOP_START = -1e20
RATES = (0.03, 0.03, 0.03, 0.8, 0.03, 0.03, 0.015, 0.8)
DECAYS = (0.1, 0.1, 0.1, 0.1, 0.1, 0.1, 0.1, 0.0)

ALL = ("x", "c", "z", "y")
LOG2E = 1.4426950408889634
BF = jnp.bfloat16
F32 = jnp.float32
FLIP = [(0, 1), (1, 0)]
CHUNK = 512
LONG = pl.CostEstimate(flops=32 * 10**9, bytes_accessed=2**24, transcendentals=0)
SHORT = pl.CostEstimate(flops=2**20, bytes_accessed=2**16, transcendentals=0)


def rope_tables(pos_rows, head_dim):
    half_dim = head_dim // 2
    frequency = THETA ** (-(jnp.arange(half_dim, dtype=F32) * 2.0 / head_dim))
    angles = pos_rows.astype(F32)[:, None] * frequency[None, :]
    cosine = jnp.cos(angles)
    sine_part = jnp.sin(angles)
    return (jnp.concatenate([cosine, cosine], -1), jnp.concatenate([sine_part, sine_part], -1))


def norm_forward(rows_in):
    inverse = lax.rsqrt(jnp.mean(rows_in * rows_in, -1, keepdims=True) + EPS)
    return (rows_in * inverse, inverse)


def norm_backward(upstream, normed, inverse, gains):
    scaled = upstream * gains
    inner = jnp.mean(scaled * normed, -1, keepdims=True)
    return (inverse * (scaled - normed * inner), jnp.sum(upstream * normed, 0))


def dot_nn(left, right):
    return lax.dot_general(left, right, (((1,), (0,)), ((), ())), preferred_element_type=F32)


def dot_tn(left, right):
    return lax.dot_general(left, right, (((0,), (0,)), ((), ())), preferred_element_type=F32)


def dot_nt(left, right):
    return lax.dot_general(left, right, (((1,), (1,)), ((), ())), preferred_element_type=F32)


def swap(values, axis):
    return lax.ppermute(values, axis, FLIP)


def hop(values, axes, step):
    return lax.ppermute(values, axes, [(i, i ^ step) for i in range(4)])


def trade(values, axes):
    return lax.all_to_all(values, axes, 0, 0, tiled=True)


def gather(values, axes):
    size = lax.axis_size(axes)
    return trade(jnp.broadcast_to(values[None], (size,) + values.shape), axes)


def pick(parts, index, dim=0):
    return lax.dynamic_index_in_dim(parts, index, dim, keepdims=False)


def gather_y(values):
    if lax.axis_size("y") == 2:
        return [values, swap(values, "y")]
    both = gather(values, "y")
    return [both[j] for j in range(both.shape[0])]


def y_places():
    size = lax.axis_size("y")
    return [lax.axis_index("y") ^ j if size == 2 else j for j in range(size)]


def scatter_y(parts):
    if lax.axis_size("y") == 2:
        me = lax.axis_index("y")
        return pick(parts, me).astype(F32) + swap(pick(parts, 1 - me).astype(BF), "y").astype(F32)
    return jnp.sum(trade(parts.astype(BF), "y").astype(F32), 0)


def tie(*values):
    return lax.optimization_barrier(values)


def by_place(pieces, me):
    return [lax.select_n(me ^ p, *pieces) for p in range(len(pieces))]


def spread(values):
    far = swap(values, "x")
    return [values, far, swap(values, "c"), swap(far, "c")]


def stack_heads(block, heads):
    return jnp.concatenate([block[:, h * HD : (h + 1) * HD] for h in range(heads)], 0)


def side_heads(block, heads):
    rows = block.shape[0] // heads
    return jnp.concatenate([block[h * rows : (h + 1) * rows] for h in range(heads)], 1)


def allowed_rows(qseg, qpos, kseg, kpos, heads):
    seen = ((kseg == qseg) | (kseg == 0)) & (kpos <= qpos)
    return jnp.concatenate([seen] * heads, 0)


def forward_kernel(flags, q_ref, k_ref, v_ref, w_ref, qs_ref, qp_ref, ks_ref, kp_ref, o_ref, l_ref, own_ref, oth_ref, acc, top, mass, *, heads, chunks):
    slot = pl.program_id(0)
    queries = stack_heads(q_ref[...], heads)
    qseg = qs_ref[:, 0:1]
    qpos = qp_ref[:, 0:1]
    acc[...] = jnp.zeros_like(acc)
    top[...] = jnp.full_like(top, TOP_START)
    mass[...] = jnp.zeros_like(mass)

    @pl.loop(0, chunks)
    def _(step):
        @pl.when(flags[slot, step] > 0)
        def _():
            start = pl.multiple_of(step * CHUNK, CHUNK)
            keys = k_ref[pl.ds(start, CHUNK), :]
            values = v_ref[pl.ds(start, CHUNK), :]
            kseg = ks_ref[pl.ds(step, 1), :]
            kpos = kp_ref[pl.ds(step, 1), :]
            scores = dot_nt(queries, keys) * (HD**-0.5 * LOG2E)
            scores = jnp.where(allowed_rows(qseg, qpos, kseg, kpos, heads), scores, NEG_BIG)
            old = top[:, 0:1]
            new = jnp.maximum(old, jnp.max(scores, -1, keepdims=True))
            weights = jnp.exp2(scores - new)
            shrink = jnp.exp2(old - new)
            mass[...] = mass[...] * shrink + jnp.sum(weights, -1, keepdims=True)
            acc[...] = acc[...] * shrink + dot_nn(weights.astype(BF), values)
            top[...] = jnp.broadcast_to(new, top.shape)

    outs = side_heads((acc[...] / mass[...]).astype(BF), heads)
    o_ref[...] = outs
    l_ref[0] = top[...] + jnp.log2(mass[...])
    part = dot_nt(outs, w_ref[...])

    @pl.when(slot < 2)
    def _():
        own_ref[0] = part

    @pl.when(slot >= 2)
    def _():
        oth_ref[0] = part.astype(BF)


def backward_kernel(flags, q_ref, k_ref, v_ref, w_ref, o_ref, l_ref, qs_ref, qp_ref, ks_ref, kp_ref, cos_ref, sin_ref, b0, b1, b2, b3, a0, a1, a2, a3, dq_ref, keep_ref, send_ref, wg_ref, bias_ref, acc, dk, dv, grad_rows, in_rows, gq, go, *, heads, chunks, shape):
    slot = pl.program_id(0)
    core = flags[4, 0]
    width = heads * HD

    @pl.when(slot == 0)
    def _():
        dk[...] = jnp.zeros_like(dk)
        dv[...] = jnp.zeros_like(dv)
        gq[...] = jnp.zeros_like(gq)
        go[...] = jnp.zeros_like(go)
        bias_ref[...] = jnp.zeros_like(bias_ref)

    for s, (b_ref, a_ref) in enumerate(((b0, a0), (b1, a1), (b2, a2), (b3, a3))):

        @pl.when(slot == s)
        def _():
            grad_rows[...] = b_ref[...]
            in_rows[...] = a_ref[...]

    queries = stack_heads(q_ref[...], heads)
    grads = stack_heads(dot_nn(grad_rows[...], w_ref[...]).astype(BF), heads)
    outs = stack_heads(o_ref[...], heads)
    delta = jnp.sum(grads.astype(F32) * outs.astype(F32), -1, keepdims=True)
    log_mass = l_ref[0][:, 0:1]
    qseg = qs_ref[:, 0:1]
    qpos = qp_ref[:, 0:1]
    acc[...] = jnp.zeros_like(acc)

    @pl.loop(0, chunks)
    def _(step):
        @pl.when(flags[slot, step] > 0)
        def _():
            start = pl.multiple_of(step * CHUNK, CHUNK)
            keys = k_ref[pl.ds(start, CHUNK), :]
            values = v_ref[pl.ds(start, CHUNK), :]
            kseg = ks_ref[pl.ds(step, 1), :]
            kpos = kp_ref[pl.ds(step, 1), :]
            scores = dot_nt(queries, keys) * (HD**-0.5 * LOG2E)
            seen = allowed_rows(qseg, qpos, kseg, kpos, heads)
            weights = jnp.exp2(jnp.where(seen, scores - log_mass, NEG_BIG))
            dv[pl.ds(start, CHUNK), :] += dot_tn(weights.astype(BF), grads)
            weight_grad = dot_nt(grads, values)
            score_grad = (weights * (weight_grad - delta)).astype(BF)
            acc[...] += dot_nn(score_grad, keys)
            dk[pl.ds(start, CHUNK), :] += dot_tn(score_grad, queries)

    rot_grad = (acc[...] * (HD**-0.5)).astype(BF).astype(F32)
    cosine = jnp.concatenate([cos_ref[...]] * heads, 0)
    sine_part = jnp.concatenate([sin_ref[...]] * heads, 0)
    back = rot_grad * cosine - pltpu.roll(rot_grad, HD // 2, 1) * sine_part
    query_grad = side_heads(back.astype(BF), heads)
    dq_ref[...] = query_grad
    bias_ref[...] += jnp.sum(query_grad.astype(F32), 0, keepdims=True)
    gq[...] += dot_tn(in_rows[...], query_grad)
    go[...] += dot_tn(grad_rows[...], o_ref[...])

    @pl.when(slot == 3)
    def _():
        wg_ref[:, :width] = gq[...].astype(BF)
        wg_ref[:, width:] = go[...].astype(BF)
        ny, nz, slots, tok = shape
        for s in range(slots):
            for k in range(nz):
                for j in range(ny):
                    at = ((s * nz + k) * ny + j) * tok
                    key_grad = dk[at : at + tok, :] * (HD**-0.5)
                    value_grad = dv[at : at + tok, :]
                    keep_ref[j, k, s] = jnp.where(core == 0, key_grad, value_grad)
                    send_ref[j, k, s] = jnp.where(core == 0, value_grad, key_grad).astype(BF)


def attend_specs(tok_rows, width, key_total, chunks):
    rows = pl.BlockSpec((tok_rows, width), lambda i, f: (i, 0))
    keys = pl.BlockSpec((key_total, HD), lambda i, f: (0, 0))
    row_info = pl.BlockSpec((tok_rows, 1), lambda i, f: (i, 0))
    key_info = pl.BlockSpec((chunks, CHUNK), lambda i, f: (0, 0))
    logs = pl.BlockSpec((1, width // HD * tok_rows, HD), lambda i, f: (i, 0, 0))
    weight = pl.BlockSpec((D, width), lambda i, f: (0, 0))
    return rows, keys, row_info, key_info, logs, weight


def attend_forward(flags, queries, keys, values, w_out_t, qseg, qpos, kseg, kpos, slots, heads):
    tok_rows = queries.shape[0] // slots
    key_total = keys.shape[0]
    chunks = key_total // CHUNK
    width = heads * HD
    stacked = heads * tok_rows
    rows, key_spec, row_info, key_info, logs, weight = attend_specs(tok_rows, width, key_total, chunks)
    return pl.pallas_call(
        functools.partial(forward_kernel, heads=heads, chunks=chunks),
        grid_spec=pltpu.PrefetchScalarGridSpec(
            num_scalar_prefetch=1,
            grid=(slots,),
            in_specs=[rows, key_spec, key_spec, weight, row_info, row_info, key_info, key_info],
            out_specs=[
                rows,
                logs,
                pl.BlockSpec((1, tok_rows, D), lambda i, f: (jnp.minimum(i, 1), 0, 0)),
                pl.BlockSpec((1, tok_rows, D), lambda i, f: (jnp.maximum(i - 2, 0), 0, 0)),
            ],
            scratch_shapes=[pltpu.VMEM((stacked, HD), F32)] * 3,
        ),
        out_shape=[
            jax.ShapeDtypeStruct((slots * tok_rows, width), BF),
            jax.ShapeDtypeStruct((slots, stacked, HD), F32),
            jax.ShapeDtypeStruct((2, tok_rows, D), F32),
            jax.ShapeDtypeStruct((2, tok_rows, D), BF),
        ],
        compiler_params=pltpu.CompilerParams(vmem_limit_bytes=40 * 2**20),
        cost_estimate=LONG,
        name="attend_forward",
    )(flags, queries, keys, values, w_out_t, qseg, qpos, kseg, kpos)


def attend_backward(flags, queries, keys, values, w_out_t, outs, logs_in, qseg, qpos, kseg, kpos, cosine, sine_part, grads, inputs, ny, nz, heads):
    slots = 4
    tok_rows = queries.shape[0] // slots
    key_total = keys.shape[0]
    chunks = key_total // CHUNK
    width = heads * HD
    stacked = heads * tok_rows
    rows, key_spec, row_info, key_info, logs, weight = attend_specs(tok_rows, width, key_total, chunks)
    turn = pl.BlockSpec((tok_rows, HD), lambda i, f: (i, 0))
    piece = pl.BlockSpec((tok_rows, D), lambda i, f: (0, 0))
    shape = (ny, nz, slots, tok_rows)
    split = pl.BlockSpec(shape + (HD,), lambda i, f: (0, 0, 0, 0, 0))
    return pl.pallas_call(
        functools.partial(backward_kernel, heads=heads, chunks=chunks, shape=shape),
        grid_spec=pltpu.PrefetchScalarGridSpec(
            num_scalar_prefetch=1,
            grid=(slots,),
            in_specs=[rows, key_spec, key_spec, weight, rows, logs, row_info, row_info, key_info, key_info, turn, turn]
            + [piece] * 8,
            out_specs=[
                rows,
                split,
                split,
                pl.BlockSpec((D, 2 * width), lambda i, f: (0, 0)),
                pl.BlockSpec((1, width), lambda i, f: (0, 0)),
            ],
            scratch_shapes=[
                pltpu.VMEM((stacked, HD), F32),
                pltpu.VMEM((key_total, HD), F32),
                pltpu.VMEM((key_total, HD), F32),
                pltpu.VMEM((tok_rows, D), BF),
                pltpu.VMEM((tok_rows, D), BF),
                pltpu.VMEM((D, width), F32),
                pltpu.VMEM((D, width), F32),
            ],
        ),
        out_shape=[
            jax.ShapeDtypeStruct((slots * tok_rows, width), BF),
            jax.ShapeDtypeStruct(shape + (HD,), F32),
            jax.ShapeDtypeStruct(shape + (HD,), BF),
            jax.ShapeDtypeStruct((D, 2 * width), BF),
            jax.ShapeDtypeStruct((1, width), F32),
        ],
        compiler_params=pltpu.CompilerParams(vmem_limit_bytes=60 * 2**20),
        cost_estimate=LONG,
        name="attend_backward",
    )(flags, queries, keys, values, w_out_t, outs, logs_in, qseg, qpos, kseg, kpos, cosine, sine_part, *grads, *inputs)


def project_kernel(core, a0, a1, a2, a3, w_ref, b_ref, cos_ref, sin_ref, q_ref, kv_ref, *, heads):
    tokens = jnp.concatenate([a0[...], a1[...], a2[...], a3[...]], 0)
    pre = dot_nn(tokens, w_ref[...]) + b_ref[...]
    cosine = cos_ref[...]
    sine_part = sin_ref[...]

    def turned(part):
        return part * cosine + pltpu.roll(part, HD // 2, 1) * sine_part

    for h in range(heads):
        q_ref[:, h * HD : (h + 1) * HD] = turned(pre[:, h * HD : (h + 1) * HD]).astype(BF)
    plain = pre[:, heads * HD :]
    kv_ref[...] = jnp.where(core[0] == 0, turned(plain), plain).astype(BF)


def whole_call(kernel, place, operands, outs, flops, name, scratch=()):
    return pl.pallas_call(
        kernel,
        in_specs=[pl.BlockSpec(memory_space=pltpu.SMEM)]
        + [pl.BlockSpec(memory_space=pltpu.VMEM)] * len(operands),
        out_specs=[pl.BlockSpec(memory_space=pltpu.VMEM)] * len(outs),
        out_shape=outs,
        scratch_shapes=list(scratch),
        compiler_params=pltpu.CompilerParams(vmem_limit_bytes=32 * 2**20),
        cost_estimate=SHORT,
        name=name,
    )(place, *operands)


def project(core, pieces, weights, bias, cosine, sine_part, heads):
    rows = 4 * pieces[0].shape[0]
    depth, width = weights.shape
    return whole_call(
        functools.partial(project_kernel, heads=heads),
        core,
        [*pieces, weights, bias, cosine, sine_part],
        [jax.ShapeDtypeStruct((rows, heads * HD), BF), jax.ShapeDtypeStruct((rows, HD), BF)],
        2 * rows * depth * width,
        "project",
    )


def finish_kernel(core, kv_ref, dq_ref, w_ref, cos_ref, sin_ref, a0, a1, a2, a3, own_ref, oth_ref, wg_ref, bias_ref):
    tok = a0.shape[0]
    parts = []
    for s in range(4):
        kept = kv_ref[2 * (core[0] ^ (s // 2)) + s % 2].astype(BF).astype(F32)
        cosine = cos_ref[s * tok : (s + 1) * tok, :]
        sine_part = sin_ref[s * tok : (s + 1) * tok, :]
        back = kept * cosine - pltpu.roll(kept, HD // 2, 1) * sine_part
        parts.append(jnp.where(core[0] == 0, back, kept).astype(BF))
    kv_grad = jnp.concatenate(parts, 0)
    bias_ref[...] = jnp.sum(kv_grad.astype(F32), 0, keepdims=True)
    tokens = jnp.concatenate([a0[...], a1[...], a2[...], a3[...]], 0)
    wg_ref[...] = dot_tn(tokens, kv_grad).astype(BF)
    both = jnp.concatenate([dq_ref[...], kv_grad], 1)
    in_grad = dot_nt(both, w_ref[...])
    own_ref[...] = in_grad[: 2 * tok].reshape(own_ref.shape)
    oth_ref[...] = in_grad[2 * tok :].astype(BF).reshape(oth_ref.shape)


def finish(core, kv_grad, query_grad, weights, cosine, sine_part, pieces):
    tok = pieces[0].shape[0]
    return whole_call(
        finish_kernel,
        core,
        [kv_grad, query_grad, weights, cosine, sine_part, *pieces],
        [
            jax.ShapeDtypeStruct((2, tok, D), F32),
            jax.ShapeDtypeStruct((2, tok, D), BF),
            jax.ShapeDtypeStruct((D, HD), BF),
            jax.ShapeDtypeStruct((1, HD), F32),
        ],
        8 * tok * D * (weights.shape[1] + HD),
        "finish",
    )


def unit_kernel(place, g_ref, u_ref, d_ref, pair_ref, down_ref):
    count, _, _, units = pair_ref.shape
    for k in range(count):
        low, high = k * units, (k + 1) * units
        pair_ref[k, 0] = g_ref[:, low:high].astype(BF)
        pair_ref[k, 1] = u_ref[:, low:high].astype(BF)
        down_ref[k, 0] = d_ref[:, low:high].astype(BF)


def unit_sets_of(place, gate, up, down, count):
    rows, units = gate.shape
    outs = [jax.ShapeDtypeStruct((count, n, rows, units // count), BF) for n in (2, 1)]
    return whole_call(unit_kernel, place, [gate, up, down], outs, 2**20, "unit_sets")


def assemble_kernel(places, *refs):
    whole = refs[-1]
    half = (len(refs) - 1) // 2
    for at in range(half):
        whole[0, places[at]] = refs[at][0]
        whole[1, places[at]] = refs[at][1]
        whole[2, places[at]] = refs[half + at][0]


def assemble_rows(places, pairs, downs):
    _, rows, units = pairs[0].shape
    out = jax.ShapeDtypeStruct((3, len(pairs), rows, units), BF)
    return whole_call(assemble_kernel, places, [*pairs, *downs], [out], 2**20, "assemble_rows")[0]


def ffn_kernel(place, p_ref, q_ref, cp_ref, cq_ref, y_ref, z_ref, cy_ref, g_ref, u_ref, d_ref, *rest):
    tok_ref, cot_ref, act_ref, dg_ref, du_ref, out_ref, in_own, in_oth = rest[-8:]
    step = pl.program_id(0)
    tok = p_ref.shape[0]
    near = jnp.where(step == 0, p_ref[...], cp_ref[...])
    far = jnp.where(step == 0, q_ref[...], cq_ref[...])
    first = place[1] == 0
    tokens = jnp.concatenate([jnp.where(first, near, far), jnp.where(first, far, near)], 0)
    y_near = jnp.where(step == 0, y_ref[0], cy_ref[0])
    y_far = jnp.where(step == 0, z_ref[0], cy_ref[1])
    cotangent = jnp.concatenate([jnp.where(first, y_near, y_far), jnp.where(first, y_far, y_near)], 0)
    gate_value = dot_nn(tokens, g_ref[0])
    up_value = dot_nn(tokens, u_ref[0])
    act_grad = dot_nn(cotangent, d_ref[0])
    sigmoid_gate = jax.nn.sigmoid(gate_value)
    silu_gate = gate_value * sigmoid_gate
    activation = (silu_gate * up_value).astype(BF)
    gate_grad = (
        act_grad * up_value * sigmoid_gate * (1.0 + gate_value * (1.0 - sigmoid_gate))
    ).astype(BF)
    up_grad = (act_grad * silu_gate).astype(BF)
    tok_ref[...] = tokens.reshape(tok_ref.shape)
    cot_ref[...] = cotangent.reshape(cot_ref.shape)
    act_ref[...] = activation.reshape(act_ref.shape)
    dg_ref[...] = gate_grad.reshape(dg_ref.shape)
    du_ref[...] = up_grad.reshape(du_ref.shape)
    out_ref[...] = dot_nt(activation, d_ref[0]).astype(BF).reshape(out_ref.shape)
    in_part = (dot_nt(gate_grad, g_ref[0]) + dot_nt(up_grad, u_ref[0])).astype(BF)
    low, high = in_part[:tok], in_part[tok:]

    def put(ref):
        ref[0] = jnp.where(first, low, high)
        ref[1] = jnp.where(first, high, low)

    @pl.when(step == 0)
    def _():
        put(in_own)

    @pl.when(step == 1)
    def _():
        put(in_oth)


def ffn_piece(place, pieces, cotangents, weights, kept):
    tok = pieces[0].shape[0]
    nz = cotangents[0].shape[0]
    units = weights.shape[-1]

    def here(width):
        return pl.BlockSpec((1, 2, 1, tok, width), lambda i, p: (i ^ p[0], 0, p[2], 0, 0))

    def matrix(at):
        return pl.BlockSpec((1, D, units), lambda i, p: (at, 0, 0))

    piece = pl.BlockSpec((tok, D), lambda i, p: (0, 0))
    cotangent = pl.BlockSpec((1, tok, D), lambda i, p: (p[2], 0, 0))
    in_spec = pl.BlockSpec((2, tok, D), lambda i, p: (0, 0, 0))
    wide = jax.ShapeDtypeStruct((2, 2, nz, tok, D), BF)
    thin = jax.ShapeDtypeStruct((2, 2, nz, tok, units), BF)
    operands = [*pieces, *cotangents, weights, weights, weights, *kept]
    results = pl.pallas_call(
        ffn_kernel,
        grid_spec=pltpu.PrefetchScalarGridSpec(
            num_scalar_prefetch=1,
            grid=(2,),
            in_specs=[piece] * 4
            + [cotangent, cotangent, in_spec, matrix(0), matrix(1), matrix(2)]
            + [pl.BlockSpec(memory_space=pl.ANY)] * len(kept),
            out_specs=[here(D), here(D), here(units), here(units), here(units), here(D), in_spec, in_spec],
        ),
        out_shape=[wide, wide, thin, thin, thin, wide]
        + [jax.ShapeDtypeStruct((2, tok, D), BF)] * 2,
        input_output_aliases={11 + i: i for i in range(len(kept))},
        compiler_params=pltpu.CompilerParams(vmem_limit_bytes=44 * 2**20),
        cost_estimate=LONG,
        name="ffn_piece",
    )(place, *operands)
    return results[:6], results[6], results[7]


def weight_kernel(place, t_ref, y_ref, a_ref, g_ref, u_ref, *outs):
    half = outs[0].shape[1]
    first = place[0] == 0
    for at, (left, right) in enumerate(((t_ref, g_ref), (t_ref, u_ref), (y_ref, a_ref))):
        grad = dot_tn(left[...], right[...]).astype(BF)
        outs[2 * at][0] = jnp.where(first, grad[:half], grad[half:])
        outs[2 * at + 1][0] = jnp.where(first, grad[half:], grad[:half])


def weight_grads(place, tokens, cotangents, act, gate_grad, up_grad, nz):
    rows = tokens.shape[0]
    units = act.shape[1]
    depth = D // nz
    wide = pl.BlockSpec((rows, depth), lambda i, p: (0, i))
    thin = pl.BlockSpec((rows, units), lambda i, p: (0, 0))
    out = pl.BlockSpec((1, depth // 2, units), lambda i, p: (i, 0, 0))
    return pl.pallas_call(
        weight_kernel,
        grid_spec=pltpu.PrefetchScalarGridSpec(
            num_scalar_prefetch=1,
            grid=(nz,),
            in_specs=[wide, wide, thin, thin, thin],
            out_specs=[out] * 6,
        ),
        out_shape=[jax.ShapeDtypeStruct((nz, depth // 2, units), BF)] * 6,
        compiler_params=pltpu.CompilerParams(vmem_limit_bytes=48 * 2**20),
        cost_estimate=LONG,
        name="weight_grads",
    )(place, tokens, cotangents, act, gate_grad, up_grad)


def adam_update(master, first, second, gradient, factor, rate, decay):
    clipped = gradient * factor
    first_new = BETA_ONE * first + (1.0 - BETA_ONE) * clipped
    second_new = BETA_TWO * second + (1.0 - BETA_TWO) * clipped * clipped
    first_hat = first_new / (1.0 - BETA_ONE**STEP)
    second_hat = second_new / (1.0 - BETA_TWO**STEP)
    master_new = master - rate * (first_hat / (jnp.sqrt(second_hat) + ADAM_EPS) + decay * master)
    return (master_new, first_new, second_new, master_new.astype(BF))


def body(
    hidden_in,
    out_grad,
    segments,
    positions,
    query_master,
    query_first,
    query_second,
    key_master,
    key_first,
    key_second,
    value_master,
    value_first,
    value_second,
    output_master,
    output_first,
    output_second,
    gate_master,
    gate_first,
    gate_second,
    up_master,
    up_first,
    up_second,
    down_master,
    down_first,
    down_second,
    small_master,
    small_first,
    small_second,
):
    nx, nc, nz, ny = (lax.axis_size(a) for a in ALL)
    ix, ic, iz, iy = (lax.axis_index(a) for a in ALL)
    nu = nx * nc
    nb = nz * ny
    me_u = ix * nc + ic
    me_b = iz * ny + iy
    tok = hidden_in.shape[0]
    qw = H * HD
    kvw = KV * HD
    heads = H // nu
    hw = heads * HD
    pack = hw + HD + hw
    rows_w = query_master.shape[0]

    q_cols = query_master.astype(BF).reshape(rows_w, nu, hw)
    k_cols = key_master.astype(BF).reshape(rows_w, nx, 1, HD)
    v_cols = value_master.astype(BF).reshape(rows_w, nx, 1, HD)
    kv_cols = jnp.concatenate([k_cols, v_cols], 2).reshape(rows_w, nu, HD)
    o_cols = output_master.astype(BF).T.reshape(rows_w, nu, hw)
    y_at = y_places()
    packed = trade(
        jnp.transpose(jnp.concatenate([q_cols, kv_cols, o_cols], -1), (1, 0, 2)), ("x", "c")
    )
    packed, small_bf, hidden_in = tie(packed, small_master.astype(BF), hidden_in)
    core = jnp.reshape(ic, (1,)).astype(jnp.int32)
    own_qkv = packed[:, :, : hw + HD]
    own_out = packed[:, :, hw + HD :]
    qkv_far = [own_qkv] + [hop(own_qkv, "z", k) for k in range(1, nz)]
    small_all = gather(small_bf, ALL).reshape(-1)

    def assemble(pieces, lead):
        whole = None
        for k, along in enumerate(pieces):
            for place, part in zip(y_at, along):
                shape = part.shape[:lead] + (1, 1) + part.shape[lead:]
                if whole is None:
                    whole = jnp.zeros(part.shape[:lead] + (nz, ny) + part.shape[lead:], BF)
                at = (0,) * lead + (iz ^ k, place) + (0,) * (part.ndim - lead)
                whole = lax.dynamic_update_slice(whole, part.reshape(shape), at)
        return whole

    qkv_far[1], qkv_far[2], qkv_far[3], out_grad, gate_master, up_master, down_rows = tie(
        *qkv_far[1:], out_grad, gate_master, up_master, down_master.T
    )
    grad_near = lax.all_gather(out_grad, "z")
    pair_sets, down_sets = unit_sets_of(core, gate_master, up_master, down_rows, nz)
    pair_all = [gather_y(pick(pair_sets, iz))]
    down_all = [gather_y(pick(down_sets, iz))]
    w_qkv = assemble([gather_y(far) for far in qkv_far], 1).reshape(D, hw + HD)


    small_vals = small_all.astype(F32).reshape(kvw, -1).T.reshape(-1)
    bias_qkv = jnp.concatenate(
        [
            lax.dynamic_slice_in_dim(small_vals, me_u * hw, hw),
            lax.dynamic_slice_in_dim(small_vals, qw + ic * kvw + ix * HD, HD),
        ]
    )
    gain_one = small_vals[qw + 2 * kvw : qw + 2 * kvw + D]
    gain_two = small_vals[qw + 2 * kvw + D :]

    slot_u = jnp.stack([(ix ^ a) * nc + (ic ^ b) for b in range(2) for a in range(2)])
    key_u = jnp.stack([(ix ^ a) * nc + b for b in range(2) for a in range(2)])
    key_b = jnp.stack([(iz ^ k) * ny + place for k in range(nz) for place in y_at])
    seg_grid = segments.reshape(nu, nb, tok)
    pos_grid = positions.reshape(nu, nb, tok)
    qseg = jnp.take(pick(seg_grid, me_b, 1), slot_u, 0)
    qpos = jnp.take(pick(pos_grid, me_b, 1), slot_u, 0)
    kseg = jnp.take(jnp.take(seg_grid, key_u, 0), key_b, 1).reshape(-1, CHUNK)
    kpos = jnp.take(jnp.take(pos_grid, key_u, 0), key_b, 1).reshape(-1, CHUNK)
    key_start = (key_u[:, None] * nb + key_b[None, :]) * tok
    key_first_index = jnp.min(key_start.reshape(-1, CHUNK // tok), -1)
    query_last_index = (slot_u * nb + me_b) * tok + tok - 1
    kseg_low, kseg_high = jnp.min(kseg, -1), jnp.max(kseg, -1)
    qseg_low, qseg_high = jnp.min(qseg, -1), jnp.max(qseg, -1)
    flags = (
        (key_first_index[None, :] <= query_last_index[:, None])
        & (
            (kseg_low[None, :] == 0)
            | (
                (kseg_low[None, :] <= qseg_high[:, None])
                & (qseg_low[:, None] <= kseg_high[None, :])
            )
        )
    ).astype(jnp.int32)
    qseg = qseg.reshape(-1, 1)
    qpos = qpos.reshape(-1, 1)
    half = HD // 2
    cosine, sine_part = rope_tables(qpos[:, 0], HD)
    sine_part = jnp.where(jnp.arange(HD)[None, :] < half, -sine_part, sine_part)

    def home(own, oth):
        came = swap(oth, "c")
        far = (own[1].astype(F32) + came[1].astype(F32)).astype(BF)
        far = swap(far, "x")
        return own[0].astype(F32) + came[0].astype(F32) + far.astype(F32), came, far

    hidden = hidden_in.astype(F32)
    normed_one, inverse_one = norm_forward(hidden)
    attn_input = spread((normed_one * gain_one).astype(BF))
    attn_input[0], grad_near = tie(attn_input[0], grad_near)
    grad_far = swap(grad_near, "x")
    queries, kv_own = project(core, attn_input, w_qkv, bias_qkv[None, :], cosine, sine_part, heads)

    def core_order(values):
        split = values.reshape(2, -1, values.shape[-1])
        return jnp.where(ic == 0, split, split[::-1]).reshape(values.shape)

    kv_own = core_order(kv_own)
    kv_far = [kv_own] + [hop(kv_own, "z", k) for k in range(1, nz)]
    kv_near = jnp.stack([far.reshape(nu, tok, HD) for far in kv_far], 1)
    kv_near, own_out, pair_sets, pair_all[0], down_all[0] = tie(
        kv_near, own_out, pair_sets, pair_all[0], down_all[0]
    )
    out_far = [own_out] + [hop(own_out, "z", k) for k in range(1, nz)]
    pair_far = [hop(pick(pair_sets, iz ^ k), "z", k) for k in range(1, nz)]
    kv_mine = jnp.stack(gather_y(kv_near), 2).reshape(-1, HD)
    kv_mine, *out_far[1:] = tie(kv_mine, *out_far[1:])
    w_out_t = assemble([gather_y(far) for far in out_far], 1).reshape(D, hw)
    kv_other = swap(kv_mine, "c")
    kv_other, down_sets, grad_far, *pair_far = tie(kv_other, down_sets, grad_far, *pair_far)
    pair_all += [gather_y(pair_far[0]), gather_y(pair_far[1])]
    down_far = [hop(pick(down_sets, iz ^ k), "z", k) for k in range(1, nz)]
    key_all = jnp.where(ic == 0, kv_mine, kv_other)
    value_all = jnp.where(ic == 0, kv_other, kv_mine)

    unit_places = jnp.stack([(iz ^ k) * ny + place for k in range(nz) for place in y_at])
    attended, logs, part_own, part_oth = attend_forward(
        flags, queries, key_all, value_all, w_out_t, qseg, qpos, kseg, kpos, nu, heads
    )
    part_oth, pair_all[1], pair_all[2], *down_far = tie(
        part_oth, pair_all[1], pair_all[2], *down_far
    )
    pair_all.append(gather_y(pair_far[2]))
    down_all += [gather_y(far) for far in down_far]
    part_came = swap(part_oth, "c")
    branch_far = swap((part_own[1] + part_came[1].astype(F32)).astype(BF), "x")
    branch = part_own[0] + part_came[0].astype(F32) + branch_far.astype(F32)
    residual = hidden + branch
    normed_two, inverse_two = norm_forward(residual)
    ffn_input = (normed_two * gain_two).astype(BF)
    near_x, near_c = swap(ffn_input, "x"), swap(ffn_input, "c")
    tok_far = [ffn_input] + [hop(ffn_input, "z", k) for k in range(1, nz)]
    tok_far[1], tok_far[2], tok_far[3], grad_far, pair_all[3], *down_all[1:] = tie(
        *tok_far[1:], grad_far, pair_all[3], *down_all[1:]
    )
    ffn_weights = assemble_rows(
        unit_places.astype(jnp.int32),
        [part for along in pair_all for part in along],
        [part for along in down_all for part in along],
    ).reshape(3, D, -1)
    pairs = [jnp.stack([pick(grad_near, iz ^ k), pick(grad_far, iz ^ k)]) for k in range(nz)]
    pairs = [swap(pair, "c") for pair in pairs]
    kept, came, far, owns = [], [], [], []
    last = nz - 1
    tok_far[0], tok_far[1], tok_far[2], tok_far[3] = tie(*tok_far)
    pieces = [[tok_far[0], near_x, near_c]]
    pieces += [[values, swap(values, "x"), swap(values, "c")] for values in tok_far[1:]]
    for k in range(nz):
        spot = jnp.stack([ic, ix, iz ^ k]).astype(jnp.int32)
        both = swap(pieces[k][1], "c")
        if k > 0:
            both, came[k - 1] = tie(both, came[k - 1])
        kept, in_own, in_oth = ffn_piece(
            spot, pieces[k] + [both], [grad_near, grad_far, pairs[k]], ffn_weights, kept
        )
        if k < last:
            in_oth, pairs[k + 1], *pieces[k + 1][1:] = tie(in_oth, pairs[k + 1], *pieces[k + 1][1:])
        if 0 < k < last:
            in_oth, far[k - 1] = tie(in_oth, far[k - 1])
        owns.append(in_own.astype(F32))
        came.append(swap(in_oth, "c"))
        far.append(swap((owns[k][1] + came[k][1].astype(F32)).astype(BF), "x"))
    backs = []
    for k in range(nz):
        back = owns[k][0] + came[k][0].astype(F32) + far[k].astype(F32)
        backs.append(back if k == 0 else hop(back.astype(BF), "z", k))
    tokens_all, cotangent_all, act_all, gate_all, up_all, out_all = kept
    out_sum = lax.psum_scatter(out_all, "c", scatter_dimension=0)
    tokens_all, far[last], out_sum = tie(tokens_all, far[last], out_sum)
    out_sum = lax.psum_scatter(out_sum, "x", scatter_dimension=0)
    units = act_all.shape[-1]
    halves = weight_grads(
        jnp.reshape(iy if ny == 2 else 0 * iy, (1,)).astype(jnp.int32),
        tokens_all.reshape(-1, D),
        cotangent_all.reshape(-1, D),
        act_all.reshape(-1, units),
        gate_all.reshape(-1, units),
        up_all.reshape(-1, units),
        nz,
    )
    halves = list(halves)
    backs[last], halves[0] = tie(backs[last], halves[0])
    ffn_in_grad = backs[0] + backs[1].astype(F32) + backs[2].astype(F32) + backs[3].astype(F32)
    norm_two_grad, gain_two_grad = norm_backward(ffn_in_grad, normed_two, inverse_two, gain_two)
    residual_grad = out_grad.astype(F32) + norm_two_grad

    def near_parts(mine, other):
        if ny == 2:
            return mine, swap(other, "y")
        both = jnp.concatenate([mine, other], 1).reshape(nz, ny, -1, units)
        return scatter_y(jnp.moveaxis(both, 1, 0)).astype(BF), None

    def near_pieces(mine, sent):
        parts = [pick(mine, iz ^ k) for k in range(nz)]
        if sent is None:
            return parts
        came = [pick(sent, iz ^ k) for k in range(nz)]
        return [(a.astype(F32) + b.astype(F32)).astype(BF) for a, b in zip(parts, came)]

    def units_side(pieces):
        return jnp.concatenate([pieces[k] for k in range(nz)], -1)

    gate_mine, gate_sent = near_parts(*halves[0:2])
    up_mine, up_sent = near_parts(*halves[2:4])
    down_mine, down_sent = near_parts(*halves[4:6])

    def heads_near(parts):
        split = jnp.transpose(parts.reshape(nu, nz, ny, rows_w, parts.shape[-1]), (2, 1, 0, 3, 4))
        return scatter_y(split)

    def heads_sum(split):
        total = pick(split, iz)
        for k in range(1, nz):
            total = total + hop(pick(split, iz ^ k).astype(BF), "z", k).astype(F32)
        return total

    branch_grad = spread(residual_grad.astype(BF))
    branch_grad[1], gate_mine = tie(branch_grad[1], gate_mine)
    gate_near = near_pieces(gate_mine, gate_sent)
    branch_grad[3], out_sum, *gate_near = tie(branch_grad[3], out_sum, *gate_near)
    out_sum = lax.psum_scatter(out_sum, "z", scatter_dimension=0)

    def units_home(pieces):
        return pieces[:1] + [hop(pieces[k], "z", k) for k in range(1, nz)]

    gate_home = units_home(gate_near)

    core_flags = jnp.concatenate([flags, jnp.full((1, flags.shape[1]), ic, jnp.int32)], 0)
    query_grad, kv_keep, kv_send, qo_grad, bias_q_grad = attend_backward(
        core_flags, queries, key_all, value_all, w_out_t, attended, logs, qseg, qpos, kseg, kpos,
        cosine, sine_part, branch_grad, attn_input, ny, nz, heads
    )
    kv_send, up_sent, down_sent, out_sum, *gate_home = tie(
        kv_send, up_sent, down_sent, out_sum, *gate_home
    )
    kv_came = swap(kv_send, "c")
    up_home = units_home(near_pieces(up_mine, up_sent))
    if ny == 2:
        kv_other = (kv_keep[1] + kv_came[1].astype(F32)).astype(BF)
        kv_other = swap(kv_other, "y")
        kv_other, qo_grad = tie(kv_other, qo_grad)
        kv_sum = kv_keep[0] + kv_came[0].astype(F32) + kv_other.astype(F32)
    else:
        kv_sum = scatter_y(kv_keep + kv_came.astype(F32))
    kv_grad = kv_sum[0]
    for k in range(1, nz):
        kv_grad = kv_grad + hop(kv_sum[k].astype(BF), "z", k).astype(F32)
    qo_near = heads_near(qo_grad)
    kv_grad, qo_near, down_sent = tie(kv_grad, qo_near, down_sent)
    down_home = units_home(near_pieces(down_mine, down_sent))
    in_own, in_oth, kv_w_grad, bias_kv_grad = finish(
        core, kv_grad, query_grad, w_qkv, cosine, sine_part, attn_input
    )
    in_oth, *gate_home = tie(in_oth, *gate_home)
    attn_in_grad, _, attn_far = home(in_own, in_oth)
    norm_one_grad, gain_one_grad = norm_backward(attn_in_grad, normed_one, inverse_one, gain_one)
    input_grad = residual_grad + norm_one_grad

    kv_w_grad, *up_home = tie(kv_w_grad, *up_home)
    kv_near = heads_near(kv_w_grad)
    total = jnp.concatenate([heads_sum(qo_near), heads_sum(kv_near)], -1).astype(BF)
    total = trade(total, ("x", "c"))
    total, attn_far, *down_home = tie(total, attn_far, *down_home)
    mixed = (residual + out_sum.astype(F32)).astype(BF)
    g_query = jnp.concatenate([total[u, :, :hw] for u in range(nu)], -1)
    g_output = jnp.concatenate([total[u, :, hw : 2 * hw] for u in range(nu)], -1).T
    g_key = jnp.concatenate([total[u, :, 2 * hw :] for u in range(0, nu, 2)], -1)
    g_value = jnp.concatenate([total[u, :, 2 * hw :] for u in range(1, nu, 2)], -1)


    bias_q_grad, bias_kv_grad = bias_q_grad[0], bias_kv_grad[0]
    bias_all = lax.dynamic_update_slice_in_dim(
        jnp.zeros((qw + 2 * kvw,), F32), bias_q_grad, me_u * hw, 0
    )
    bias_all = lax.dynamic_update_slice_in_dim(
        bias_all, bias_kv_grad, qw + ic * kvw + ix * HD, 0
    )
    small_ordered = jnp.concatenate([bias_all, gain_one_grad, gain_two_grad])
    small_grad = small_ordered.reshape(-1, kvw).T.reshape(nu * nb, -1)
    g_small = jnp.sum(trade(small_grad, ALL), 0)
    g_query, g_key, g_value, g_output = (
        lax.optimization_barrier(g).astype(F32) for g in (g_query, g_key, g_value, g_output)
    )
    local_squares = jnp.float32(0.0)
    for part in (g_query, g_key, g_value, g_output, g_small, *gate_home, *up_home, *down_home):
        wide = part.astype(F32)
        local_squares = local_squares + jnp.sum(wide * wide)
    homes = gate_home + up_home + list(down_home)
    local_squares, mixed, *homes = tie(local_squares, mixed, *homes)
    g_gate, g_up, g_down = (
        lax.optimization_barrier(units_side(by_place(homes[at : at + nz], iz)))
        for at in (0, nz, 2 * nz)
    )
    g_gate, g_up, g_down = g_gate.astype(F32), g_up.astype(F32), g_down.T.astype(F32)
    shards = (g_query, g_key, g_value, g_output, g_gate, g_up, g_down, g_small)
    squares = trade(jnp.full((nu * nb, HD), local_squares, F32), ALL)
    grad_norm = jnp.sqrt(jnp.sum(squares[:, 0]))
    factor = CLIP / jnp.maximum(grad_norm, CLIP)
    masters = (query_master, key_master, value_master, output_master, gate_master, up_master, down_master, small_master)
    firsts = (query_first, key_first, value_first, output_first, gate_first, up_first, down_first, small_first)
    seconds = (query_second, key_second, value_second, output_second, gate_second, up_second, down_second, small_second)
    results = [mixed, input_grad, grad_norm]
    for slot in range(8):
        results.extend(
            adam_update(
                masters[slot],
                firsts[slot],
                seconds[slot],
                shards[slot],
                factor,
                RATES[slot],
                DECAYS[slot],
            )
        )
    return tuple(results)


def solution(mesh):
    ulysses, blk = mesh.devices.shape
    fine = Mesh(mesh.devices.reshape(2, ulysses // 2, 4, blk // 4), ALL)
    rows = P(ALL, None)
    cols = P(None, ALL)
    wide = P(("z", "y"), ("x", "c"))
    tall = P(("x", "c"), ("z", "y"))
    flat = P(ALL)
    in_specs = (rows, rows, P(), P()) + (rows,) * 9 + (cols,) * 3 + (wide,) * 6 + (tall,) * 3 + (flat,) * 3
    out_specs = (rows, rows, P()) + (rows,) * 12 + (cols,) * 4 + (wide,) * 8 + (tall,) * 4 + (flat,) * 4
    return jax.shard_map(body, mesh=fine, in_specs=in_specs, out_specs=out_specs, check_vma=False)
```

time: 1960 us -> 706 us (0.36)
  waiting for transfers between devices: 1300 us -> 250 us
  blocking collectives: 304 us -> 0 us
  matrix products: 199 us -> 0 us
  starting transfers between devices: 12.4 us -> 142 us
  Pallas kernels: 0 us -> 124 us
  local copies, waits for them, and re-layouts: 23.7 us -> 56.6 us
    reduce_scatter x11 -> x3, waiting for transfers between devices: 930 us -> 12.5 us  [the longest x1 12.4 us: body(): out_sum = lax.psum_scatter(out_sum, 'z', scatter_dimension=0)]
    all_gather x9 -> x1, waiting for transfers between devices: 350 us -> 17.2 us  [body(): grad_near = lax.all_gather(out_grad, 'z')]
    ppermute x0 -> x99, waiting for transfers between devices: none -> 209 us  [the longest x39 111 us: hop(): return lax.ppermute(values, axes, [(i, i ^ step) for i in range(4)])]
    dot_general x49 -> x0, matrix products: 199 us -> none  [the longest x7 40.2 us: contract_rows(): lax.dot_general(left, right, (((0,), (0,)), ((), ())), preferred_element_...]
    all_gather x2 -> x0, blocking collectives: 141 us -> none  [the longest x1 71.5 us: body(): lax.all_gather(key_master.astype(jnp.bfloat16), ('ulysses', 'blk'), axis=...]
    pallas_call x0 -> x11, Pallas kernels: none -> 124 us  [the longest x4 53.8 us: ffn_piece(): pl.pallas_call(ffn_kernel, grid_spec=pltpu.PrefetchScalarGridSpec(num_sca...]
    ppermute x0 -> x99, starting transfers between devices: none -> 118 us  [the longest x39 78.6 us: hop(): return lax.ppermute(values, axes, [(i, i ^ step) for i in range(4)])]
    unnamed x2 -> x0, blocking collectives: 82.4 us -> none
  transfers between devices with their start and end apart: 23 -> 108, of which waited for: 19 -> 40; matrix products, arithmetic and copies ran while one was open for 9% -> 12% of each run, Pallas kernels for 0% -> 16%
where the time goes in v1:
time: 706 us; the launch traced here: 697 us
  waiting for transfers between devices  250 us (35%)
  starting transfers between devices  142 us (20%)
  Pallas kernels  124 us (18%)
  other arithmetic  95.3 us (13%)
  local copies, waits for them, and re-layouts  56.6 us (8%)
  between operations  29.1 us (4%)
    ppermute x39, waiting for transfers between devices, hop(): return lax.ppermute(values, axes, [(i, i ^ step) for i in range(4)])  111 us
    ppermute x60, waiting for transfers between devices, swap(): return lax.ppermute(values, axis, FLIP)  98.8 us
    ppermute x39, starting transfers between devices, hop(): return lax.ppermute(values, axes, [(i, i ^ step) for i in range(4)])  78.6 us
    pallas_call x4, Pallas kernels, ffn_piece(): pl.pallas_call(ffn_kernel, grid_spec=pltpu.PrefetchScalarGridSpec(num_sca...  53.8 us
    ppermute x60, starting transfers between devices, swap(): return lax.ppermute(values, axis, FLIP)  39.4 us
    pallas_call x1, Pallas kernels, attend_backward(): pl.pallas_call(functools.partial(backward_kernel, heads=heads, chunks=chu...  27.3 us
    all_to_all x5, starting transfers between devices, trade(): return lax.all_to_all(values, axes, 0, 0, tiled=True)  24.2 us
    unnamed x276, local copies, waits for them, and re-layouts  21.2 us
  transfers between devices with their start and end apart: 108, of which 40 were waited for; matrix products, arithmetic and copies ran while one was open for 12% of the time, Pallas kernels for 16%

profile of v1, /device:TPU:0, one launch (start us, length us, event | category | flops | bytes accessed | tf_op | source)
XLA Modules:
  0.0 696.9 jit_solution(2903715058056634513)
XLA Ops:
  11.8 4.3 all-to-all-start
  35.2 5.3 all-to-all-start.1
  41.9 10.6 %all-to-all-done.1 = bf16[32,1,160]{2,1,0:T(2,128)(2,1)S(1)} async-done(((bf16[32,1,160]{2,1,0:T(2,128)(2,1)}), bf16[32,1,160]{2,1,0:T(2,128)(2,1)S(1)}, u32[]{:S(2)}, u32[]{:S(2)}) %all-to-all-start.1) | async-done | bytes 10272 | tf_op jit(solution)/shard_map/all_to_all | solution.py:80
  73.9 17.2 %all-gather.3.cloned.1.call-done = bf16[512,1536]{1,0:T(8,128)(2,1)} async-done(((bf16[128,1536]{1,0:T(8,128)(2,1)}), bf16[512,1536]{1,0:T(8,128)(2,1)}) %all-gather.3.cloned.1.call-update) | async-done | bytes 1572880 | tf_op jit(solution)/shard_map/all_gather | solution.py:647
  118.0 9.5 %collective-permute-done.15 = bf16[4,4,128,128]{3,2,1,0:T(8,128)(2,1)S(1)} collective-permute-done((bf16[4,4,128,128]{3,2,1,0:T(8,128)(2,1)S(1)}, bf16[4,4,128,128]{3,2,1,0:T(8,128)(2,1)S(1)}, u32[]{:S(2)}, u32[]{:S(2)}) %collective-permute-start.15) | collective-permute-done | bytes 524320 | tf_op jit(solution)/shard_map/ppermute | solution.py:72
  138.6 4.4 collective-permute-done.27
  144.2 27.1 %collective-permute-done.22.refs_4_ = bf16[2,192,560]{2,1,0:T(8,128)(2,1)S(1)} collective-permute-done((bf16[2,192,560]{2,1,0:T(8,128)(2,1)S(1)}, bf16[2,192,560]{2,1,0:T(8,128)(2,1)S(1)}, u32[]{:S(2)}, u32[]{:S(2)}) %collective-permute-start.22) | collective-permute-done | bytes 430112 | tf_op jit(solution)/shard_map/ppermute | solution.py:76
  178.8 14.4 %attend_forward.1 = (bf16[512,384]{1,0:T(8,128)(2,1)S(1)}, f32[4,384,128]{2,1,0:T(8,128)S(1)}, f32[2,128,1536]{2,1,0:T(8,128)S(1)}, bf16[2,128,1536]{2,1,0:T(8,128)(2,1)S(1)}) custom-call(s32[4,8]{1,0:T(4,128)S(1)} %and_convert_fusion.flags, bf16[512,384]{1,0:T(8,128)(2,1)S(1)} %copy-done.53, bf16[4096,128]{1,0:T(8,128)(2,1)S(1)} %get-tuple-element.467.k_ref, ...), custom_call_target="tpu_custom_call" | custom-call | flops 32000000000 | bytes 16777216 | tf_op jit(solution)/shard_map/attend_forward/pallas_call | solution.py:269
  202.1 7.9 %collective-permute-done.34 = bf16[128,1536]{1,0:T(8,128)(2,1)} collective-permute-done((bf16[128,1536]{1,0:T(8,128)(2,1)}, bf16[128,1536]{1,0:T(8,128)(2,1)}, u32[]{:S(2)}, u32[]{:S(2)}) %collective-permute-start.34) | collective-permute-done | bytes 393248 | tf_op jit(solution)/shard_map/ppermute | solution.py:72
  211.9 4.4 collective-permute-start.37
  219.5 6.3 collective-permute-done.40.refs_13_
  229.0 19.6 %collective-permute-done.36.p_ref = bf16[128,1536]{1,0:T(8,128)(2,1)S(1)} collective-permute-done((bf16[128,1536]{1,0:T(8,128)(2,1)S(1)}, bf16[128,1536]{1,0:T(8,128)(2,1)S(1)}, u32[]{:S(2)}, u32[]{:S(2)}) %collective-permute-start.36) | collective-permute-done | bytes 393248 | tf_op jit(solution)/shard_map/ppermute | solution.py:76
  257.6 13.4 %ffn_piece.4 = (bf16[2,2,4,128,1536]{4,3,2,1,0:T(8,128)(2,1)}, bf16[2,2,4,128,1536]{4,3,2,1,0:T(8,128)(2,1)}, bf16[2,2,4,128,560]{4,3,2,1,0:T(8,128)(2,1)S(1)}, ...) custom-call(s32[3]{0:T(128)S(1)} %get-tuple-element.532.place, ...), custom_call_target="tpu_custom_call" | custom-call | flops 32000000000 | bytes 16777216 | tf_op jit(solution)/shard_map/ffn_piece/pallas_call | solution.py:512
  274.7 13.6 %ffn_piece.5 = (bf16[2,2,4,128,1536]{4,3,2,1,0:T(8,128)(2,1)}, bf16[2,2,4,128,1536]{4,3,2,1,0:T(8,128)(2,1)}, bf16[2,2,4,128,560]{4,3,2,1,0:T(8,128)(2,1)S(1)}, ...) custom-call(s32[3]{0:T(128)S(1)} %get-tuple-element.449.place, ...), custom_call_target="tpu_custom_call", output_to_operand_aliasing={{0}: (11, {}), {1}: (12, {}), {2}: (13, {}), {3}: (14, {}),... | custom-call | flops 32000000000 | bytes 16777216 | tf_op jit(solution)/shard_map/ffn_piece/pallas_call | solution.py:512
  295.3 13.3 %ffn_piece.6 = (bf16[2,2,4,128,1536]{4,3,2,1,0:T(8,128)(2,1)}, bf16[2,2,4,128,1536]{4,3,2,1,0:T(8,128)(2,1)}, bf16[2,2,4,128,560]{4,3,2,1,0:T(8,128)(2,1)S(1)}, ...) custom-call(s32[3]{0:T(128)S(1)} %get-tuple-element.533.place, ...), custom_call_target="tpu_custom_call", output_to_operand_aliasing={{0}: (11, {}), {1}: (12, {}), {2}: (13, {}), {3}: (14, {}),... | custom-call | flops 32000000000 | bytes 16777216 | tf_op jit(solution)/shard_map/ffn_piece/pallas_call | solution.py:512
  315.0 13.4 %ffn_piece.7 = (bf16[2,2,4,128,1536]{4,3,2,1,0:T(8,128)(2,1)}, bf16[2,2,4,128,1536]{4,3,2,1,0:T(8,128)(2,1)}, bf16[2,2,4,128,560]{4,3,2,1,0:T(8,128)(2,1)S(1)}, ...) custom-call(s32[3]{0:T(128)S(1)} %get-tuple-element.534.place, ...), custom_call_target="tpu_custom_call", output_to_operand_aliasing={{0}: (11, {}), {1}: (12, {}), {2}: (13, {}), {3}: (14, {}),... | custom-call | flops 32000000000 | bytes 16777216 | tf_op jit(solution)/shard_map/ffn_piece/pallas_call | solution.py:512
  337.7 9.2 %collective-permute-done.67 = bf16[128,1536]{1,0:T(8,128)(2,1)} collective-permute-done((bf16[128,1536]{1,0:T(8,128)(2,1)S(1)}, bf16[128,1536]{1,0:T(8,128)(2,1)}, u32[]{:S(2)}, u32[]{:S(2)}) %collective-permute-start.67) | collective-permute-done | bytes 393248 | tf_op jit(solution)/shard_map/ppermute | solution.py:72
  348.7 6.0 collective-permute-done.64
  360.7 20.4 %weight_grads.1 = (bf16[4,192,560]{2,1,0:T(8,128)(2,1)S(1)}, bf16[4,192,560]{2,1,0:T(8,128)(2,1)S(1)}, bf16[4,192,560]{2,1,0:T(8,128)(2,1)S(1)}, bf16[4,192,560]...) custom-call(s32[1]{0:T(128)} %bitcast.100.place, ...), custom_call_target="tpu_custom_call" | custom-call | flops 32000000000 | bytes 16777216 | tf_op jit(solution)/shard_map/weight_grads/pallas_call | solution.py:548
  389.0 9.8 %collective-permute-done.69.b1 = bf16[128,1536]{1,0:T(8,128)(2,1)S(1)} collective-permute-done((bf16[128,1536]{1,0:T(8,128)(2,1)}, bf16[128,1536]{1,0:T(8,128)(2,1)S(1)}, u32[]{:S(2)}, u32[]{:S(2)}) %collective-permute-start.69) | collective-permute-done | bytes 393248 | tf_op jit(solution)/shard_map/ppermute | solution.py:72
  399.3 4.4 collective-permute-done.72
  407.6 13.3 %collective-permute-start.75 = (bf16[192,560]{1,0:T(8,128)(2,1)}, bf16[192,560]{1,0:T(8,128)(2,1)}, u32[]{:S(2)}, u32[]{:S(2)}) collective-permute-start(bf16[192,560]{1,0:T(8,128)(2,1)} %get-tuple-element.352), channel_id=1, source_target_pairs={{0,2},{2,0},{4,6},{6,4},{1,3},{3,1},{5,7},{7,5},{8,10},{10,8},{12,... | collective-permute-start | bytes 645128 | tf_op jit(solution)/shard_map/ppermute | solution.py:76
  423.2 27.3 %attend_backward.1 = (bf16[512,384]{1,0:T(8,128)(2,1)}, f32[2,4,4,128,128]{4,3,2,1,0:T(8,128)}, bf16[2,4,4,128,128]{4,3,2,1,0:T(8,128)(2,1)}, bf16[1536,768]{1,0:T(8,128)(2,1)}, f32[1,384]{1,0:T(1,128)}) custom-call(s32[5,8]{1,0:T(8,128)} %concatenate.54.flags, bf16[512,384]{1,0:T(8,128)(2,1)} %copy-done.52, bf16[4096,128]{1,0:T(8,128)(2,1)} %copy-done.18, ...), custom_call_target="tpu_custom_call" | custom-call | flops 32000000000 | bytes 16777216 | tf_op jit(solution)/shard_map/attend_backward/pallas_call | solution.py:307
  454.5 12.4 %reduce-scatter.8.cloned.1.call-done = bf16[1,128,1536]{2,1,0:T(8,128)(2,1)} async-done(((bf16[4,128,1536]{2,1,0:T(8,128)(2,1)}), bf16[1,128,1536]{2,1,0:T(8,128)(2,1)}) %reduce-scatter.8.cloned.1.call-update) | async-done | bytes 393232 | tf_op jit(solution)/shard_map/reduce_scatter | solution.py:834
  473.5 13.6 %collective-permute-done.79 = bf16[4,4,128,128]{3,2,1,0:T(8,128)(2,1)} collective-permute-done((bf16[4,4,128,128]{3,2,1,0:T(8,128)(2,1)}, bf16[4,4,128,128]{3,2,1,0:T(8,128)(2,1)}, u32[]{:S(2)}, u32[]{:S(2)}) %collective-permute-start.79) | collective-permute-done | bytes 524320 | tf_op jit(solution)/shard_map/ppermute | solution.py:72
  507.1 11.7 %collective-permute-start.87 = (bf16[192,560]{1,0:T(8,128)(2,1)S(1)}, bf16[192,560]{1,0:T(8,128)(2,1)S(1)}, u32[]{:S(2)}, u32[]{:S(2)}) collective-permute-start(bf16[192,560]{1,0:T(8,128)(2,1)S(1)} %get-tuple-element.474), channel_id=1, source_target_pairs={{0,2},{2,0},{4,6},{6,4},{1,3},{3,1},{5,7},{7,5},{8,10},{10,8},{12,... | collective-permute-start | bytes 645128 | tf_op jit(solution)/shard_map/ppermute | solution.py:76
  526.0 5.2 collective-permute-done.88
  553.1 23.2 %collective-permute-done.92 = bf16[4,48,128]{2,1,0:T(8,128)(2,1)S(1)} collective-permute-done((bf16[4,48,128]{2,1,0:T(8,128)(2,1)S(1)}, bf16[4,48,128]{2,1,0:T(8,128)(2,1)S(1)}, u32[]{:S(2)}, u32[]{:S(2)}) %collective-permute-start.92) | collective-permute-done | bytes 49184 | tf_op jit(solution)/shard_map/ppermute | solution.py:76
  588.7 6.5 collective-permute-done.98
  595.3 11.3 %collective-permute-done.97 = bf16[192,560]{1,0:T(8,128)(2,1)} collective-permute-done((bf16[192,560]{1,0:T(8,128)(2,1)}, bf16[192,560]{1,0:T(8,128)(2,1)}, u32[]{:S(2)}, u32[]{:S(2)}) %collective-permute-start.97) | collective-permute-done | bytes 215072 | tf_op jit(solution)/shard_map/ppermute | solution.py:76
  613.9 4.3 all-to-all-start.3
  647.4 6.0 all-to-all-start.4
  (671 shorter events, 298.0 us)
Async XLA Ops:
  27.7 37.5 %collective-permute-start.6 = (bf16[4,48,512]{2,1,0:T(8,128)(2,1)}, bf16[4,48,512]{2,1,0:T(8,128)(2,1)}, u32[]{:S(2)}, u32[]{:S(2)}) collective-permute-start(bf16[4,48,512]{2,1,0:T(8,128)(2,1)} %slice.153), channel_id=1, source_target_pairs={{0,1},{1,0},{2,3},{3,2},{4,5},{5,4},{6,7},{7,6},{8,9},{9,8},{10,11... | collective-permute-start | bytes 589832 | tf_op jit(solution)/shard_map/ppermute | solution.py:72
  30.0 24.6 %collective-permute-start.2 = (bf16[4,48,512]{2,1,0:T(8,128)(2,1)}, bf16[4,48,512]{2,1,0:T(8,128)(2,1)}, u32[]{:S(2)}, u32[]{:S(2)}) collective-permute-start(bf16[4,48,512]{2,1,0:T(8,128)(2,1)} %slice.153), channel_id=1, source_target_pairs={{0,6},{2,4},{4,2},{6,0},{1,7},{3,5},{5,3},{7,1},{8,14},{10,12},{12... | collective-permute-start | bytes 589832 | tf_op jit(solution)/shard_map/ppermute | solution.py:76
  40.5 50.6 %all-gather.3.cloned.1.call-start = ((), (), s32[]{:S(2)}) async-start(), calls=%async_computation.11 | async-start | bytes 1966080 | tf_op jit(solution)/shard_map/all_gather | solution.py:647
  54.7 292.2 %reduce-scatter.4.cloned.1.call-start = ((), (), s32[]{:S(2)}) async-start(), calls=%async_computation.8 | async-start | bytes 9437184 | tf_op jit(solution)/shard_map/reduce_scatter | solution.py:781
  56.6 34.5 %collective-permute-start.4 = (bf16[128,1536]{1,0:T(8,128)(2,1)}, bf16[128,1536]{1,0:T(8,128)(2,1)}, u32[]{:S(2)}, u32[]{:S(2)}) collective-permute-start(bf16[128,1536]{1,0:T(8,128)(2,1)} %fusion.8.a0), channel_id=1, source_target_pairs={{0,8},{8,0},{1,9},{9,1},{2,10},{10,2},{3,11},{11,3},{4,12},{12,4},... | collective-permute-start | bytes 1179656 | tf_op jit(solution)/shard_map/ppermute | solution.py:72
  68.5 42.6 %collective-permute-start.14 = (bf16[1,192,560]{2,1,0:T(8,128)(2,1)}, bf16[1,192,560]{2,1,0:T(8,128)(2,1)}, u32[]{:S(2)}, u32[]{:S(2)}) collective-permute-start(bf16[1,192,560]{2,1,0:T(8,128)(2,1)} %dynamic-slice_bitcast_fusion.7.refs_8_), channel_id=1, source_target_pairs={{0,1},{1,0},{2,3},{3,2},{4,5},{5,4},{6,7},{7,6},{8,9},{9,8},{10,11... | collective-permute-start | bytes 645128 | tf_op jit(solution)/shard_map/ppermute | solution.py:72
  70.2 40.9 %collective-permute-start.13 = (bf16[2,192,560]{2,1,0:T(8,128)(2,1)}, bf16[2,192,560]{2,1,0:T(8,128)(2,1)}, u32[]{:S(2)}, u32[]{:S(2)}) collective-permute-start(bf16[2,192,560]{2,1,0:T(8,128)(2,1)} %dynamic-slice_bitcast_fusion.3.refs_0_), channel_id=1, source_target_pairs={{0,1},{1,0},{2,3},{3,2},{4,5},{5,4},{6,7},{7,6},{8,9},{9,8},{10,11... | collective-permute-start | bytes 1290248 | tf_op jit(solution)/shard_map/ppermute | solution.py:72
  104.9 66.5 %collective-permute-start.20 = (bf16[4,128,1536]{2,1,0:T(8,128)(2,1)}, bf16[4,128,1536]{2,1,0:T(8,128)(2,1)}, u32[]{:S(2)}, u32[]{:S(2)}) collective-permute-start(bf16[4,128,1536]{2,1,0:T(8,128)(2,1)} %bitcast.347), channel_id=1, source_target_pairs={{0,16},{16,0},{1,17},{17,1},{2,18},{18,2},{3,19},{19,3},{4,20},{20... | collective-permute-start | bytes 4718600 | tf_op jit(solution)/shard_map/ppermute | solution.py:72
  130.2 41.2 %collective-permute-start.22 = (bf16[2,192,560]{2,1,0:T(8,128)(2,1)S(1)}, bf16[2,192,560]{2,1,0:T(8,128)(2,1)S(1)}, u32[]{:S(2)}, u32[]{:S(2)}) collective-permute-start(bf16[2,192,560]{2,1,0:T(8,128)(2,1)S(1)} %get-tuple-element.481), channel_id=1, source_target_pairs={{0,4},{2,6},{4,0},{6,2},{1,5},{3,7},{5,1},{7,3},{8,12},{10,14},{12... | collective-permute-start | bytes 1290248 | tf_op jit(solution)/shard_map/ppermute | solution.py:76
  136.2 35.1 %collective-permute-start.19 = (bf16[4096,128]{1,0:T(8,128)(2,1)S(1)}, bf16[4096,128]{1,0:T(8,128)(2,1)S(1)}, u32[]{:S(2)}, u32[]{:S(2)}) collective-permute-start(bf16[4096,128]{1,0:T(8,128)(2,1)S(1)} %bitcast.359), channel_id=1, source_target_pairs={{0,8},{8,0},{1,9},{9,1},{2,10},{10,2},{3,11},{11,3},{4,12},{12,4},... | collective-permute-start | bytes 3145736 | tf_op jit(solution)/shard_map/ppermute | solution.py:72
  143.0 28.4 %collective-permute-start.21 = (bf16[2,192,560]{2,1,0:T(8,128)(2,1)S(1)}, bf16[2,192,560]{2,1,0:T(8,128)(2,1)S(1)}, u32[]{:S(2)}, u32[]{:S(2)}) collective-permute-start(bf16[2,192,560]{2,1,0:T(8,128)(2,1)S(1)} %get-tuple-element.482), channel_id=1, source_target_pairs={{0,2},{2,0},{4,6},{6,4},{1,3},{3,1},{5,7},{7,5},{8,10},{10,8},{12,... | collective-permute-start | bytes 1290248 | tf_op jit(solution)/shard_map/ppermute | solution.py:76
  216.2 32.4 %collective-permute-start.36 = (bf16[128,1536]{1,0:T(8,128)(2,1)S(1)}, bf16[128,1536]{1,0:T(8,128)(2,1)S(1)}, u32[]{:S(2)}, u32[]{:S(2)}) collective-permute-start(bf16[128,1536]{1,0:T(8,128)(2,1)S(1)} %multiply_convert_fusion.p_ref), channel_id=1, source_target_pairs={{0,4},{2,6},{4,0},{6,2},{1,5},{3,7},{5,1},{7,3},{8,12},{10,14},{12... | collective-permute-start | bytes 1179656 | tf_op jit(solution)/shard_map/ppermute | solution.py:76
  216.3 32.4 %collective-permute-start.35 = (bf16[128,1536]{1,0:T(8,128)(2,1)S(1)}, bf16[128,1536]{1,0:T(8,128)(2,1)S(1)}, u32[]{:S(2)}, u32[]{:S(2)}) collective-permute-start(bf16[128,1536]{1,0:T(8,128)(2,1)S(1)} %multiply_convert_fusion.p_ref), channel_id=1, source_target_pairs={{0,2},{2,0},{4,6},{6,4},{1,3},{3,1},{5,7},{7,5},{8,10},{10,8},{12,... | collective-permute-start | bytes 1179656 | tf_op jit(solution)/shard_map/ppermute | solution.py:76
  225.8 25.1 %collective-permute-start.42 = (bf16[128,1536]{1,0:T(8,128)(2,1)S(1)}, bf16[128,1536]{1,0:T(8,128)(2,1)S(1)}, u32[]{:S(2)}, u32[]{:S(2)}) collective-permute-start(bf16[128,1536]{1,0:T(8,128)(2,1)S(1)} %multiply_convert_fusion.p_ref), channel_id=1, source_target_pairs={{0,16},{16,0},{1,17},{17,1},{2,18},{18,2},{3,19},{19,3},{4,20},{20... | collective-permute-start | bytes 1179656 | tf_op jit(solution)/shard_map/ppermute | solution.py:72
  331.8 73.2 %reduce-scatter.6.cloned.1.call-start = ((), (), s32[]{:S(2)}) async-start(), calls=%async_computation.9 | async-start | bytes 4718592 | tf_op jit(solution)/shard_map/reduce_scatter | solution.py:783
  346.9 120.0 %reduce-scatter.8.cloned.1.call-start = ((), (), s32[]{:S(2)}) async-start(), calls=%async_computation.10 | async-start | bytes 1966080 | tf_op jit(solution)/shard_map/reduce_scatter | solution.py:834
  348.6 32.8 %collective-permute-start.61 = (bf16[128,1536]{1,0:T(8,128)(2,1)S(1)}, bf16[128,1536]{1,0:T(8,128)(2,1)S(1)}, u32[]{:S(2)}, u32[]{:S(2)}) collective-permute-start(bf16[128,1536]{1,0:T(8,128)(2,1)S(1)} %fusion.26), channel_id=1, source_target_pairs={{0,2},{2,0},{4,6},{6,4},{1,3},{3,1},{5,7},{7,5},{8,10},{10,8},{12,... | collective-permute-start | bytes 1179656 | tf_op jit(solution)/shard_map/ppermute | solution.py:76
  356.6 29.1 %collective-permute-start.65 = (bf16[128,1536]{1,0:T(8,128)(2,1)S(1)}, bf16[128,1536]{1,0:T(8,128)(2,1)S(1)}, u32[]{:S(2)}, u32[]{:S(2)}) collective-permute-start(bf16[128,1536]{1,0:T(8,128)(2,1)S(1)} %fusion.22), channel_id=1, source_target_pairs={{0,4},{2,6},{4,0},{6,2},{1,5},{3,7},{5,1},{7,3},{8,12},{10,14},{12... | collective-permute-start | bytes 1179656 | tf_op jit(solution)/shard_map/ppermute | solution.py:76
  405.6 44.9 %collective-permute-start.73 = (bf16[4,192,560]{2,1,0:T(8,128)(2,1)}, bf16[4,192,560]{2,1,0:T(8,128)(2,1)}, u32[]{:S(2)}, u32[]{:S(2)}) collective-permute-start(bf16[4,192,560]{2,1,0:T(8,128)(2,1)} %copy-done.50), channel_id=1, source_target_pairs={{0,1},{1,0},{2,3},{3,2},{4,5},{5,4},{6,7},{7,6},{8,9},{9,8},{10,11... | collective-permute-start | bytes 2580488 | tf_op jit(solution)/shard_map/ppermute | solution.py:72
  406.1 44.4 %collective-permute-start.74 = (bf16[4,192,560]{2,1,0:T(8,128)(2,1)}, bf16[4,192,560]{2,1,0:T(8,128)(2,1)}, u32[]{:S(2)}, u32[]{:S(2)}) collective-permute-start(bf16[4,192,560]{2,1,0:T(8,128)(2,1)} %copy-done.49), channel_id=1, source_target_pairs={{0,1},{1,0},{2,3},{3,2},{4,5},{5,4},{6,7},{7,6},{8,9},{9,8},{10,11... | collective-permute-start | bytes 2580488 | tf_op jit(solution)/shard_map/ppermute | solution.py:72
  407.6 42.9 %collective-permute-start.75 = (bf16[192,560]{1,0:T(8,128)(2,1)}, bf16[192,560]{1,0:T(8,128)(2,1)}, u32[]{:S(2)}, u32[]{:S(2)}) collective-permute-start(bf16[192,560]{1,0:T(8,128)(2,1)} %get-tuple-element.352), channel_id=1, source_target_pairs={{0,2},{2,0},{4,6},{6,4},{1,3},{3,1},{5,7},{7,5},{8,10},{10,8},{12,... | collective-permute-start | bytes 645128 | tf_op jit(solution)/shard_map/ppermute | solution.py:76
  420.9 33.6 %collective-permute-start.76 = (bf16[192,560]{1,0:T(8,128)(2,1)}, bf16[192,560]{1,0:T(8,128)(2,1)}, u32[]{:S(2)}, u32[]{:S(2)}) collective-permute-start(bf16[192,560]{1,0:T(8,128)(2,1)} %get-tuple-element.353), channel_id=1, source_target_pairs={{0,4},{2,6},{4,0},{6,2},{1,5},{3,7},{5,1},{7,3},{8,12},{10,14},{12... | collective-permute-start | bytes 645128 | tf_op jit(solution)/shard_map/ppermute | solution.py:76
  421.7 32.8 %collective-permute-start.77 = (bf16[192,560]{1,0:T(8,128)(2,1)}, bf16[192,560]{1,0:T(8,128)(2,1)}, u32[]{:S(2)}, u32[]{:S(2)}) collective-permute-start(bf16[192,560]{1,0:T(8,128)(2,1)} %get-tuple-element.354), channel_id=1, source_target_pairs={{0,6},{2,4},{4,2},{6,0},{1,7},{3,5},{5,3},{7,1},{8,14},{10,12},{12... | collective-permute-start | bytes 645128 | tf_op jit(solution)/shard_map/ppermute | solution.py:76
  491.1 30.2 %collective-permute-start.83 = (bf16[4,4,48,768]{3,2,1,0:T(8,128)(2,1)}, bf16[4,4,48,768]{3,2,1,0:T(8,128)(2,1)}, u32[]{:S(2)}, u32[]{:S(2)}) collective-permute-start(bf16[4,4,48,768]{3,2,1,0:T(8,128)(2,1)} %bitcast.330), channel_id=1, source_target_pairs={{0,1},{1,0},{2,3},{3,2},{4,5},{5,4},{6,7},{7,6},{8,9},{9,8},{10,11... | collective-permute-start | bytes 3538952 | tf_op jit(solution)/shard_map/ppermute | solution.py:72
  503.1 28.1 %collective-permute-start.88 = (bf16[192,560]{1,0:T(8,128)(2,1)S(1)}, bf16[192,560]{1,0:T(8,128)(2,1)S(1)}, u32[]{:S(2)}, u32[]{:S(2)}) collective-permute-start(bf16[192,560]{1,0:T(8,128)(2,1)S(1)} %get-tuple-element.473), channel_id=1, source_target_pairs={{0,4},{2,6},{4,0},{6,2},{1,5},{3,7},{5,1},{7,3},{8,12},{10,14},{12... | collective-permute-start | bytes 645128 | tf_op jit(solution)/shard_map/ppermute | solution.py:76
  537.1 39.4 %collective-permute-start.94 = (bf16[2,128,1536]{2,1,0:T(8,128)(2,1)S(1)}, bf16[2,128,1536]{2,1,0:T(8,128)(2,1)S(1)}, u32[]{:S(2)}, u32[]{:S(2)}) collective-permute-start(bf16[2,128,1536]{2,1,0:T(8,128)(2,1)S(1)} %get-tuple-element.373), channel_id=1, source_target_pairs={{0,8},{8,0},{1,9},{9,1},{2,10},{10,2},{3,11},{11,3},{4,12},{12,4},... | collective-permute-start | bytes 2359304 | tf_op jit(solution)/shard_map/ppermute | solution.py:72
  545.6 30.7 %collective-permute-start.84 = (bf16[4,48,768]{2,1,0:T(8,128)(2,1)S(1)}, bf16[4,48,768]{2,1,0:T(8,128)(2,1)S(1)}, u32[]{:S(2)}, u32[]{:S(2)}) collective-permute-start(bf16[4,48,768]{2,1,0:T(8,128)(2,1)S(1)} %get-tuple-element.461), channel_id=1, source_target_pairs={{0,2},{2,0},{4,6},{6,4},{1,3},{3,1},{5,7},{7,5},{8,10},{10,8},{12,... | collective-permute-start | bytes 884744 | tf_op jit(solution)/shard_map/ppermute | solution.py:76
  546.7 29.7 %collective-permute-start.86 = (bf16[4,48,768]{2,1,0:T(8,128)(2,1)S(1)}, bf16[4,48,768]{2,1,0:T(8,128)(2,1)S(1)}, u32[]{:S(2)}, u32[]{:S(2)}) collective-permute-start(bf16[4,48,768]{2,1,0:T(8,128)(2,1)S(1)} %get-tuple-element.462), channel_id=1, source_target_pairs={{0,6},{2,4},{4,2},{6,0},{1,7},{3,5},{5,3},{7,1},{8,14},{10,12},{12... | collective-permute-start | bytes 884744 | tf_op jit(solution)/shard_map/ppermute | solution.py:76
  548.5 27.9 %collective-permute-start.85 = (bf16[4,48,768]{2,1,0:T(8,128)(2,1)S(1)}, bf16[4,48,768]{2,1,0:T(8,128)(2,1)S(1)}, u32[]{:S(2)}, u32[]{:S(2)}) collective-permute-start(bf16[4,48,768]{2,1,0:T(8,128)(2,1)S(1)} %get-tuple-element.463), channel_id=1, source_target_pairs={{0,4},{2,6},{4,0},{6,2},{1,5},{3,7},{5,1},{7,3},{8,12},{10,14},{12... | collective-permute-start | bytes 884744 | tf_op jit(solution)/shard_map/ppermute | solution.py:76
  549.1 27.2 %collective-permute-start.92 = (bf16[4,48,128]{2,1,0:T(8,128)(2,1)S(1)}, bf16[4,48,128]{2,1,0:T(8,128)(2,1)S(1)}, u32[]{:S(2)}, u32[]{:S(2)}) collective-permute-start(bf16[4,48,128]{2,1,0:T(8,128)(2,1)S(1)} %get-tuple-element.513), channel_id=1, source_target_pairs={{0,4},{2,6},{4,0},{6,2},{1,5},{3,7},{5,1},{7,3},{8,12},{10,14},{12... | collective-permute-start | bytes 147464 | tf_op jit(solution)/shard_map/ppermute | solution.py:76
  577.6 29.0 %collective-permute-start.95 = (bf16[128,1536]{1,0:T(8,128)(2,1)}, bf16[128,1536]{1,0:T(8,128)(2,1)}, u32[]{:S(2)}, u32[]{:S(2)}) collective-permute-start(bf16[128,1536]{1,0:T(8,128)(2,1)} %fusion.38), channel_id=1, source_target_pairs={{0,16},{16,0},{1,17},{17,1},{2,18},{18,2},{3,19},{19,3},{4,20},{20... | collective-permute-start | bytes 1179656 | tf_op jit(solution)/shard_map/ppermute | solution.py:72
  578.3 28.2 %all-to-all-start.2 = ((bf16[4,48,896]{2,1,0:T(8,128)(2,1)}), bf16[4,48,896]{2,1,0:T(8,128)(2,1)}, u32[]{:S(2)}, u32[]{:S(2)}) async-start(bf16[4,48,896]{2,1,0:T(8,128)(2,1)} %pad_maximum_fusion.6), calls=%async_computation.5 | async-start | bytes 688128 | tf_op jit(solution)/shard_map/all_to_all | solution.py:80
  (213 other events, 2863.0 us)
Sparse Core Ops, SparseCore 0:
  54.8 36.3 all-gather.2
  331.9 13.2 reduce-scatter.3
  347.6 45.0 reduce-scatter.5
  405.1 61.7 reduce-scatter.7
